TPU v7x, 128 devices: a whole 4x4x4 slice. The times are simulated.
128 devices in a mesh: cube: 8 (over y_lo, z), row: 4 (over x), col: 4 (over y_hi, core).
Axes of the slice: x: 4, y: 4 (y_hi: 2, y_lo: 2; y = y_hi * 2 + y_lo), z: 4, core: 2. Of those that a mesh axis runs over, the one named last changes fastest.
Arguments:
- front_entries: float32 [8, 6144, 6144], P('cube', 'row', 'col')
- child_update: float32 [8, 3072, 3072], P('cube', 'row', 'col')
- block_map: int32 [8, 2, 24], P('cube'), may hold values from 0 to 47, as said below
Outputs:
- factored: float32 [8, 6144, 6144], P('cube', 'row', 'col')
Inputs may be any that keep to these rules, and one draw needn't show every extreme that they name: `block_map`: for each front and child the 24 entries are distinct. Among the child blocks of one device (blocks t * 3072 / 512 to the next such bound) at most 2 go to parent blocks of one grid row, parent block // (6144 / 512); some go exactly 2.
All inputs are finite; a program needn't handle non-finite values.
Results may differ from a plain program's by a relative error of at most 0.0001.
Values sent between devices are 32-bit elements; how exact they have to be, the bound alone decides.
No kernel may reach another device: no remote copies, remote signals or barrier semaphores. Data moves between devices by JAX's collectives and lax.ppermute only.
A program may use at most 192 MiB of HBM per device.

v0:
```python
import jax
import jax.numpy as jnp
from jax import lax
from jax.sharding import PartitionSpec as P

BLK = 128
CAP = 2
PW = 256
PANELS = 2


def swapped(block, axis, distance):
    count = lax.axis_size(axis)
    route = []
    for low in range(count):
        high = low | 1 << distance
        if high != low and high < count:
            route += [(low, high), (high, low)]
    return lax.ppermute(block, axis, route)


def spread(x, axis, root):
    mine = lax.axis_index(axis) == root
    return lax.psum(jnp.where(mine, x, jnp.zeros_like(x)), axis)


def slot_table(parent_blocks, child_local, parent_local):
    count = parent_blocks.shape[0]
    block_ids = jnp.arange(count)
    sender = block_ids // child_local
    target_row = parent_blocks // parent_local
    local_block = parent_blocks % parent_local
    earlier = (
        (sender[:, None] == sender[None, :])
        & (target_row[:, None] == target_row[None, :])
        & (block_ids[None, :] < block_ids[:, None])
    )
    rank_same = jnp.sum(earlier.astype(jnp.int32), axis=1)
    return (sender, target_row, rank_same, local_block)


def sender_onehot(tables, device_index, child_local, slot_total):
    sender, target_row, rank_same, local_block = tables
    mine_target = lax.dynamic_slice_in_dim(target_row, device_index * child_local, child_local)
    mine_rank = lax.dynamic_slice_in_dim(rank_same, device_index * child_local, child_local)
    slot_of = mine_target * CAP + mine_rank
    return (jnp.arange(slot_total)[:, None] == slot_of[None, :]).astype(jnp.float32)


def receiver_onehot(tables, device_index, parent_local, slot_total):
    sender, target_row, rank_same, local_block = tables
    arriving = target_row == device_index
    place_hot = (
        (local_block[:, None] == jnp.arange(parent_local)[None, :]) & arriving[:, None]
    ).astype(jnp.float32)
    slot_hot = ((sender * CAP + rank_same)[:, None] == jnp.arange(slot_total)[None, :]).astype(
        jnp.float32
    )
    return jnp.dot(
        place_hot.T, slot_hot, precision=lax.Precision.HIGHEST, preferred_element_type=jnp.float32
    )


def solve_rows(pivot_factor, rows_in):
    return jax.scipy.linalg.solve_triangular(pivot_factor, rows_in.T, lower=True).T


def shards(front_entries, child_update, block_map):
    highest = lax.Precision.HIGHEST
    front_now = front_entries[0]
    own_update = child_update[0]
    block_maps = block_map[0]
    local_rows = front_now.shape[0]
    local_child = own_update.shape[0]
    row_count = lax.axis_size("row")
    child_local = local_child // BLK
    parent_local = local_rows // BLK
    slot_total = row_count * CAP
    row_here = lax.axis_index("row")
    col_here = lax.axis_index("col")
    sibling = swapped(own_update, "cube", 0)
    stacked = jnp.stack([own_update, sibling])
    tables = [
        slot_table(block_maps[0], child_local, parent_local),
        slot_table(block_maps[1], child_local, parent_local),
    ]
    send_rows = jnp.stack(
        [sender_onehot(entry, row_here, child_local, slot_total) for entry in tables]
    )
    send_cols = jnp.stack(
        [sender_onehot(entry, col_here, child_local, slot_total) for entry in tables]
    )
    take_rows = jnp.stack(
        [receiver_onehot(entry, row_here, parent_local, slot_total) for entry in tables]
    )
    take_cols = jnp.stack(
        [receiver_onehot(entry, col_here, parent_local, slot_total) for entry in tables]
    )
    blocks_in = stacked.reshape(2, child_local, BLK, child_local, BLK)
    packed = jnp.einsum("cxk,ckaqb->cxaqb", send_rows, blocks_in, precision=highest)
    packed = jnp.einsum("cyq,cxaqb->cxayb", send_cols, packed, precision=highest)
    packed = packed.reshape(2, slot_total * BLK, slot_total * BLK)
    arrived = lax.all_to_all(
        lax.all_to_all(packed, "row", split_axis=1, concat_axis=1, tiled=True),
        "col",
        split_axis=2,
        concat_axis=2,
        tiled=True,
    )
    arrived = arrived.reshape(2, slot_total, BLK, slot_total, BLK)
    placed = jnp.einsum("cps,csatb->cpatb", take_rows, arrived, precision=highest)
    added = jnp.einsum("cqt,cpatb->paqb", take_cols, placed, precision=highest)
    front_now = front_now + added.reshape(local_rows, local_rows)
    row_global = row_here * local_rows + jnp.arange(local_rows)
    col_global = col_here * local_rows + jnp.arange(local_rows)
    for panel_index in range(PANELS):
        start_col = panel_index * PW
        stop_col = start_col + PW
        column = spread(front_now[:, start_col:stop_col], "col", 0)
        diagonal = spread(column[start_col:stop_col], "row", 0)
        pivot_factor = jnp.linalg.cholesky(diagonal)
        lower_rows = jnp.where(
            row_global[:, None] >= start_col, solve_rows(pivot_factor, column), 0.0
        )
        lower_cols = spread(lower_rows, "row", col_here)
        trail_rows = jnp.where(row_global[:, None] >= stop_col, lower_rows, 0.0)
        trail_cols = jnp.where(col_global[:, None] >= stop_col, lower_cols, 0.0)
        front_now = front_now - jnp.dot(
            trail_rows, trail_cols.T, precision=highest, preferred_element_type=jnp.float32
        )
        front_now = front_now.at[:, start_col:stop_col].set(
            jnp.where(col_here == 0, lower_rows, front_now[:, start_col:stop_col])
        )
        upper_band = front_now[start_col:stop_col]
        front_now = front_now.at[start_col:stop_col].set(
            jnp.where((row_here == 0) & (col_global[None, :] >= stop_col), 0.0, upper_band)
        )
    return front_now[None]


def solution(mesh):
    in_specs = (P("cube", "row", "col"), P("cube", "row", "col"), P("cube", None, None))
    out_specs = P("cube", "row", "col")
    return jax.shard_map(shards, mesh=mesh, in_specs=in_specs, out_specs=out_specs, check_vma=False)
```

profile of v0, /device:TPU:85, one launch (start us, length us, event | category | flops | bytes accessed | tf_op | source)
XLA Modules:
  0.0 877.4 jit_solution(1864679166128016114)
XLA Ops:
  13.9 45.0 %collective-permute-done = f32[768,768]{1,0:T(8,128)} collective-permute-done((f32[768,768]{1,0:T(8,128)}, f32[768,768]{1,0:T(8,128)}, u32[]{:S(2)}, u32[]{:S(2)}) %collective-permute-start) | collective-permute-done | bytes 2359328 | tf_op jit(solution)/shard_map/ppermute | solution.py:19
  73.4 9.3 %reshape.472 = f32[2,1024,1024]{2,1,0:T(8,128)} reshape(f32[2,8,128,8,128]{4,3,2,1,0:T(8,128)} %fusion.8) | data formatting | bytes 16777216 | tf_op jit(solution)/shard_map/reshape | solution.py:102
  82.7 14.4 %copy.66 = f32[2,1024,1024]{2,0,1:T(2,128)S(1)} copy(f32[2,1024,1024]{2,1,0:T(8,128)} %reshape.472) | data formatting | bytes 16777216 | tf_op jit(solution)/shard_map/reshape | solution.py:102
  97.1 93.3 %all_to_all.10 = f32[2,1024,1024]{2,0,1:T(2,128)} all-to-all(f32[2,1024,1024]{2,0,1:T(2,128)S(1)} %copy.66), channel_id=1, replica_groups=mesh['cube'=8,'row'=4,'col'=4] {'row'}, dimensions={1} | all-to-all | bytes 16777216 | tf_op jit(solution)/shard_map/all_to_all | solution.py:104
  190.4 17.0 %copy.67 = f32[2,1024,1024]{1,0,2:T(2,128)} copy(f32[2,1024,1024]{2,0,1:T(2,128)} %all_to_all.10) | data formatting | bytes 16777216 | tf_op jit(solution)/shard_map/all_to_all | solution.py:104
  207.4 9.1 %all-to-all-start.1 = ((f32[2,1024,1024]{1,0,2:T(2,128)}), f32[2,1024,1024]{1,0,2:T(2,128)}, u32[]{:S(2)}, u32[]{:S(2)}) async-start(f32[2,1024,1024]{1,0,2:T(2,128)} %copy.67), calls=%async_computation.1 | async-start | bytes 16777216 | tf_op jit(solution)/shard_map/all_to_all | solution.py:103
  216.6 9.6 %copy.62 = f32[1,1536,1536]{1,2,0:T(8,128)} copy(f32[1,1536,1536]{2,1,0:T(8,128)} %param.14) | data formatting | bytes 18874368 | tf_op args[0]
  227.2 80.6 %all-to-all-done.1 = f32[2,1024,1024]{1,0,2:T(2,128)} async-done(((f32[2,1024,1024]{1,0,2:T(2,128)}), f32[2,1024,1024]{1,0,2:T(2,128)}, u32[]{:S(2)}, u32[]{:S(2)}) %all-to-all-start.1) | async-done | bytes 8388640 | tf_op jit(solution)/shard_map/all_to_all | solution.py:103
  307.9 11.5 %reshape.502 = f32[2,8,128,8,128]{2,1,0,4,3:T(8,128)} reshape(f32[2,1024,1024]{1,0,2:T(2,128)} %all-to-all-done.1) | data formatting | bytes 16777216 | tf_op jit(solution)/shard_map/reshape | solution.py:110
  319.3 8.7 copy.69
  328.1 17.5 %fusion.56 = f32[2,12,128,8,128]{4,1,3,2,0:T(8,128)} fusion(f32[2,8,128,8,128]{4,1,3,2,0:T(8,128)} %copy.69, f32[1,12,8]{1,2,0:T(8,128)S(1)} %convolution_bitcast_fusion.2, f32[1,12,8]{1,2,0:T(8,128)S(1)} %convolution_bitcast_fusion.3), kind=kOutput, calls=%fused_computation.104 | convolution fusion | flops 301990080 | bytes 20972288 | tf_op jit(solution)/shard_map/cps,csatb->cpatb/dot_general | solution.py:111
  345.6 19.0 %fusion = f32[12,128,128,12,1]{2,3,4,1,0:T(8,128)S(1)} fusion(f32[2,12,128,8,128]{4,1,3,2,0:T(8,128)} %fusion.56, f32[1,12,8]{1,2,0:T(8,128)S(1)} %convolution_bitcast_fusion, f32[1,12,8]{1,2,0:T(8,128)S(1)} %convolution_bitcast_fusion.1), kind=kOutput, calls=%fused_computation.4 | convolution fusion | flops 452985024 | bytes 22020864 | tf_op jit(solution)/shard_map/cqt,cpatb->paqb/dot_general | solution.py:112
  364.6 8.4 copy.105
  373.0 9.6 %copy.71 = f32[1536,1536]{0,1:T(8,128)} copy(f32[1536,1536]{1,0:T(8,128)} %bitcast.159) | data formatting | bytes 18874368 | tf_op jit(solution)/shard_map/reshape | solution.py:113
  382.6 12.4 %bitcast_add_fusion = f32[1536,1536]{0,1:T(8,128)} fusion(f32[1536,1536]{0,1:T(8,128)} %copy.71, f32[1,1536,1536]{1,2,0:T(8,128)} %copy.62), kind=kLoop, calls=%fused_computation.9 | loop fusion | flops 2359296 | bytes 28311552 | tf_op jit(solution)/shard_map/add | solution.py:113
  397.8 52.9 %all-reduce.8.cloned.1.call-done = f32[1536,256]{0,1:T(8,128)} async-done(((f32[1536,256]{0,1:T(8,128)}), f32[1536,256]{0,1:T(8,128)}) %all-reduce.8.cloned.1.call-update) | async-done | bytes 1572880 | tf_op jit(solution)/shard_map/psum | solution.py:24
  452.7 40.1 %all-reduce.10.cloned.1.call-done = f32[256,256]{0,1:T(8,128)} async-done(((f32[256,256]{0,1:T(8,128)}), f32[256,256]{0,1:T(8,128)}) %all-reduce.10.cloned.1.call-update) | async-done | bytes 262160 | tf_op jit(solution)/shard_map/psum | solution.py:24
  494.8 11.7 %cholesky.130 = f32[128,128]{1,0:T(8,128)S(1)} custom-call(f32[128,128]{1,0:T(8,128)S(1)} %cholesky.194), custom_call_target="Cholesky" | custom-call | tf_op jit(solution)/shard_map/jit(cholesky)/cholesky | solution.py:121
  506.6 9.8 %custom-call.13 = f32[1,128,128]{1,2,0:T(8,128)S(1)} custom-call(f32[1,128,128]{2,1,0:T(8,128)S(1)} %get-tuple-element.104), custom_call_target="InvertDiagBlocksLowerTriangular" | custom-call | tf_op jit(solution)/shard_map/jit(cholesky)/cholesky | solution.py:121
  516.9 11.7 %cholesky.147 = f32[128,128]{1,0:T(8,128)S(1)} custom-call(f32[128,128]{1,0:T(8,128)S(1)} %convolution_subtract_fusion.5), custom_call_target="Cholesky" | custom-call | tf_op jit(solution)/shard_map/jit(cholesky)/cholesky | solution.py:121
  535.8 19.7 %custom-call.14 = f32[2,128,128]{1,2,0:T(8,128)S(1)} custom-call(f32[2,128,128]{2,1,0:T(8,128)S(1)} %get-tuple-element.69), custom_call_target="InvertDiagBlocksLowerTriangular" | custom-call | tf_op jit(solution)/shard_map/jit(_solve_triangular)/triangular_solve | solution.py:65
  560.0 51.0 %all-reduce.12.cloned.1.call-done = f32[1536,256]{0,1:T(8,128)} async-done(((f32[1536,256]{0,1:T(8,128)}), f32[1536,256]{0,1:T(8,128)}) %all-reduce.12.cloned.1.call-update) | async-done | bytes 1572880 | tf_op jit(solution)/shard_map/psum | solution.py:24
  611.0 11.4 %convolution_subtract_fusion.1 = f32[1536,1536]{0,1:T(8,128)S(1)} fusion(f32[1536,1536]{0,1:T(8,128)} %bitcast_add_fusion, f32[1536,256]{0,1:T(8,128)} %all-reduce.12.cloned.1.call-done, f32[128,1536]{1,0:T(8,128)S(1)} %fusion.41, f32[128,1536]{1,0:T(8,128)S(1)} %fusion.24, pred[1536]{0:T(1024)(128)(4,1)S(1)} %fusion.62, pred[1536]{0:T(1024)(128)(4,1)S(1)} %fusion.64, ...), kind=kOutput, calls=%fused_computation.7 | convolution fusion | flops 7251689472 | bytes 22024704 | tf_op jit(solution)/shard_map/dot_general | solution.py:128
  628.8 52.0 %all-reduce.14.cloned.1.call-done = f32[1536,256]{0,1:T(8,128)} async-done(((f32[1536,256]{0,1:T(8,128)}), f32[1536,256]{0,1:T(8,128)}) %all-reduce.14.cloned.1.call-update) | async-done | bytes 1572880 | tf_op jit(solution)/shard_map/psum | solution.py:24
  682.7 40.1 %all-reduce.16.cloned.1.call-done = f32[256,256]{0,1:T(8,128)} async-done(((f32[256,256]{0,1:T(8,128)}), f32[256,256]{0,1:T(8,128)}) %all-reduce.16.cloned.1.call-update) | async-done | bytes 262160 | tf_op jit(solution)/shard_map/psum | solution.py:24
  724.9 11.7 %cholesky.164 = f32[128,128]{1,0:T(8,128)S(1)} custom-call(f32[128,128]{1,0:T(8,128)S(1)} %cholesky.197), custom_call_target="Cholesky" | custom-call | tf_op jit(solution)/shard_map/jit(cholesky)/cholesky | solution.py:121
  736.6 9.8 %custom-call.15 = f32[1,128,128]{1,2,0:T(8,128)S(1)} custom-call(f32[1,128,128]{2,1,0:T(8,128)S(1)} %get-tuple-element.100), custom_call_target="InvertDiagBlocksLowerTriangular" | custom-call | tf_op jit(solution)/shard_map/jit(cholesky)/cholesky | solution.py:121
  746.9 11.7 %cholesky.181 = f32[128,128]{1,0:T(8,128)S(1)} custom-call(f32[128,128]{1,0:T(8,128)S(1)} %convolution_subtract_fusion.4), custom_call_target="Cholesky" | custom-call | tf_op jit(solution)/shard_map/jit(cholesky)/cholesky | solution.py:121
  765.5 19.7 %custom-call.16 = f32[2,128,128]{1,2,0:T(8,128)S(1)} custom-call(f32[2,128,128]{2,1,0:T(8,128)S(1)} %get-tuple-element.70), custom_call_target="InvertDiagBlocksLowerTriangular" | custom-call | tf_op jit(solution)/shard_map/jit(_solve_triangular)/triangular_solve | solution.py:65
  792.1 51.1 %all-reduce.18.cloned.1.call-done = f32[1536,256]{0,1:T(8,128)} async-done(((f32[1536,256]{0,1:T(8,128)}), f32[1536,256]{0,1:T(8,128)}) %all-reduce.18.cloned.1.call-update) | async-done | bytes 1572880 | tf_op jit(solution)/shard_map/psum | solution.py:24
  843.2 11.4 %convolution_subtract_fusion = f32[1536,1536]{0,1:T(8,128)S(1)} fusion(f32[1536,1536]{0,1:T(8,128)} %copy-done, f32[256,1536]{1,0:T(8,128)S(1)} %copy.78, f32[1536,256]{0,1:T(8,128)} %all-reduce.18.cloned.1.call-done, pred[1536]{0:T(1024)(128)(4,1)S(1)} %fusion.61, pred[1536]{0:T(1024)(128)(4,1)S(1)} %fusion.63), kind=kOutput, calls=%fused_computation.6 | convolution fusion | flops 7250903040 | bytes 22023168 | tf_op jit(solution)/shard_map/dot_general | solution.py:128
  860.7 9.6 %copy.80 = f32[1,1536,1536]{2,1,0:T(8,128)} copy(f32[1,1536,1536]{1,2,0:T(8,128)} %fusion.14) | data formatting | bytes 18874368 | tf_op jit(solution)/shard_map/scatter | solution.py:135
  (116 shorter events, 77.7 us)
Async XLA Ops:
  6.5 52.4 %collective-permute-start = (f32[768,768]{1,0:T(8,128)}, f32[768,768]{1,0:T(8,128)}, u32[]{:S(2)}, u32[]{:S(2)}) collective-permute-start(f32[768,768]{1,0:T(8,128)} %bitcast.160), channel_id=1, source_target_pairs={{0,16},{16,0},{32,48},{48,32},{64,80},{80,64},{96,112},{112,96},{1... | collective-permute-start | bytes 7077896 | tf_op jit(solution)/shard_map/ppermute | solution.py:19
  10.4 3.1 copy-start.5
  61.5 1.9 copy-start.1
  207.4 100.4 %all-to-all-start.1 = ((f32[2,1024,1024]{1,0,2:T(2,128)}), f32[2,1024,1024]{1,0,2:T(2,128)}, u32[]{:S(2)}, u32[]{:S(2)}) async-start(f32[2,1024,1024]{1,0,2:T(2,128)} %copy.67), calls=%async_computation.1 | async-start | bytes 16777216 | tf_op jit(solution)/shard_map/all_to_all | solution.py:103
  216.5 234.1 %all-reduce.8.cloned.1.call-start = ((), (), s32[]{:S(2)}) async-start(), calls=%async_computation.2 | async-start | bytes 3145728 | tf_op jit(solution)/shard_map/psum | solution.py:24
  397.7 95.0 %all-reduce.10.cloned.1.call-start = ((), (), s32[]{:S(2)}) async-start(), calls=%async_computation.3 | async-start | bytes 524288 | tf_op jit(solution)/shard_map/psum | solution.py:24
  452.4 158.6 %all-reduce.12.cloned.1.call-start = ((), (), s32[]{:S(2)}) async-start(), calls=%async_computation.4 | async-start | bytes 3145728 | tf_op jit(solution)/shard_map/psum | solution.py:24
  494.8 60.6 %copy-start.3 = (f32[1536,256]{0,1:T(8,128)S(1)}, f32[1536,256]{0,1:T(8,128)}, u32[]{:S(2)}) copy-start(f32[1536,256]{0,1:T(8,128)} %all-reduce.8.cloned.1.call-done) | copy-start | bytes 4718596
  559.3 121.4 %all-reduce.14.cloned.1.call-start = ((), (), s32[]{:S(2)}) async-start(), calls=%async_computation.5 | async-start | bytes 3145728 | tf_op jit(solution)/shard_map/psum | solution.py:24
  623.7 3.7 copy-start
  628.7 94.1 %all-reduce.16.cloned.1.call-start = ((), (), s32[]{:S(2)}) async-start(), calls=%async_computation.6 | async-start | bytes 524288 | tf_op jit(solution)/shard_map/psum | solution.py:24
  682.4 160.7 %all-reduce.18.cloned.1.call-start = ((), (), s32[]{:S(2)}) async-start(), calls=%async_computation.7 | async-start | bytes 3145728 | tf_op jit(solution)/shard_map/psum | solution.py:24
  724.8 60.4 %copy-start.4 = (f32[1536,256]{0,1:T(8,128)S(1)}, f32[1536,256]{0,1:T(8,128)}, u32[]{:S(2)}) copy-start(f32[1536,256]{0,1:T(8,128)} %all-reduce.14.cloned.1.call-done) | copy-start | bytes 4718596
  788.0 1.4 copy-start.2
Sparse Core Ops, SparseCore 0:
  397.8 52.8 all-reduce.7
  453.0 39.6 all-reduce.9
  559.4 51.5 all-reduce.11
  628.8 51.8 all-reduce.13
  683.0 39.7 all-reduce.15
  791.6 51.5 all-reduce.17
where the time goes:
time: 892 us; the launch traced here: 877 us
  waiting for transfers between devices  413 us (46%)
  other arithmetic  139 us (16%)
  local copies, waits for them, and re-layouts  127 us (14%)
  blocking collectives  93.3 us (10%)
  matrix products  76.6 us (9%)
  between operations  16.7 us (2%)
  starting transfers between devices  11.1 us (1%)
    psum x6, waiting for transfers between devices, spread(): return lax.psum(jnp.where(mine, x, jnp.zeros_like(x)), axis)  287 us
    all_to_all x1, blocking collectives, shards(): lax.all_to_all(packed, 'row', split_axis=1, concat_axis=1, tiled=True)  93.3 us
    all_to_all x1, waiting for transfers between devices, shards(): lax.all_to_all(lax.all_to_all(packed, 'row', split_axis=1, concat_axis=1,...  80.6 us
    another operation x14, other arithmetic, shards(): pivot_factor = jnp.linalg.cholesky(diagonal)  69.3 us
    ppermute x1, waiting for transfers between devices, swapped(): return lax.ppermute(block, axis, route)  45 us
    another operation x5, other arithmetic, solve_rows(): jax.scipy.linalg.solve_triangular(pivot_factor, rows_in.T, lower=True)  39.4 us
    unnamed x15, local copies, waits for them, and re-layouts  25.9 us
    reshape x2, local copies, waits for them, and re-layouts, shards(): packed = packed.reshape(2, slot_total * BLK, slot_total * BLK)  23.7 us
  transfers between devices with their start and end apart: 8, of which 8 were waited for; matrix products, arithmetic and copies ran while one was open for 2% of the time, Pallas kernels for 0%

commit v1 on v0

v1 whole, which is shorter than its diff:
```python
import functools
import jax
import jax.numpy as jnp
from jax import lax
from jax.experimental import pallas as pl
from jax.experimental.pallas import tpu as pltpu
from jax.sharding import PartitionSpec as P

BLK = 128
CAP = 2
PW = 256
ROWS = 4
CB = 6
PB = 12
OWN = 2
HIGHEST = lax.Precision.HIGHEST
ANY = pl.BlockSpec(memory_space=pl.ANY)
SMEM = pl.BlockSpec(memory_space=pltpu.SMEM)
VMEM = pl.BlockSpec(memory_space=pltpu.VMEM)
F32 = jnp.float32
TICK = jax.ShapeDtypeStruct((8, BLK), F32)


def params(mb=56):
    return pltpu.CompilerParams(vmem_limit_bytes=mb << 20)


def cost(flops, nbytes):
    return pl.CostEstimate(flops=flops, bytes_accessed=nbytes, transcendentals=0)


def ranked(meta, base, sender):
    vals = [meta[base + CB * sender + i] for i in range(CB)]
    targets = [lax.div(v, PB) for v in vals]
    ranks = []
    for i in range(CB):
        rank = jnp.int32(0)
        for j in range(i):
            rank = rank + (targets[j] == targets[i]).astype(jnp.int32)
        ranks.append(rank)
    places = [v - PB * t for v, t in zip(vals, targets)]
    return targets, ranks, places


def place_of(meta, base, q):
    found = jnp.int32(-1)
    for j in range(ROWS * CB):
        found = jnp.where(meta[base + j] == q, jnp.int32(j), found)
    return found


def pack_kernel(base, meta, child, _, out, sems):
    rt, rr, _ = ranked(meta, base, meta[0])
    ct, cr, _ = ranked(meta, base, meta[1])
    copies = []
    for i in range(CB):
        for j in range(CB):
            slot = (rt[i] * ROWS + ct[j]) * 4 + rr[i] * CAP + cr[j]
            copies.append(
                pltpu.make_async_copy(
                    child.at[pl.ds(i * BLK, BLK), pl.ds(j * BLK, BLK)],
                    out.at[slot],
                    sems.at[i * CB + j],
                )
            )
            copies[-1].start()
    for c in copies:
        c.wait()


def pack(meta, child, base, tick):
    return pl.pallas_call(
        functools.partial(pack_kernel, base),
        out_shape=jax.ShapeDtypeStruct((64, BLK, BLK), F32),
        in_specs=[SMEM, VMEM, ANY],
        out_specs=ANY,
        scratch_shapes=[pltpu.SemaphoreType.DMA((CB * CB,))],
        compiler_params=params(),
        cost_estimate=cost(0, 1 << 20),
    )(meta, child, tick)


def strips_kernel(meta, child, sibling, keep, send, sems):
    s = meta[1]
    k = lax.rem(s, 2)
    copies = []
    for hi in range(2):
        for m, source in enumerate((child, sibling)):
            for which, out in ((0, keep), (1, send)):
                q = 2 * hi + lax.rem(k + which, 2)
                j = place_of(meta, OWN + 24 * m, q) - CB * s
                j = jnp.clip(j, 0, CB - 1)
                copies.append(
                    pltpu.make_async_copy(
                        source.at[:, pl.ds(pl.multiple_of(j * BLK, BLK), BLK)],
                        out.at[hi, m],
                        sems.at[hi * 4 + m * 2 + which],
                    )
                )
                copies[-1].start()
    for c in copies:
        c.wait()


def strips(meta, child, sibling):
    shape = jax.ShapeDtypeStruct((2, 2, CB * BLK, BLK), F32)
    return pl.pallas_call(
        strips_kernel,
        out_shape=(shape, shape),
        in_specs=[SMEM, VMEM, VMEM],
        out_specs=(ANY, ANY),
        scratch_shapes=[pltpu.SemaphoreType.DMA((8,))],
        compiler_params=params(),
        cost_estimate=cost(0, 1 << 20),
    )(meta, child, sibling)


def choose_kernel(meta, keep, got, out, sems):
    s = meta[1]
    k = lax.rem(s, 2)
    h = 1 - lax.div(s, 2)
    for m in range(2):
        j = place_of(meta, OWN + 24 * m, 2 * h + k)
        src = lax.rem(lax.div(jnp.maximum(j, 0), CB), 2)

        @pl.when(src == k)
        def _():
            pltpu.make_async_copy(keep.at[h, m], out.at[m], sems.at[m]).start()

        @pl.when(src != k)
        def _():
            pltpu.make_async_copy(got.at[h, m], out.at[m], sems.at[m]).start()

    for m in range(2):
        pltpu.make_async_copy(keep.at[0, m], out.at[m], sems.at[m]).wait()


def choose(meta, keep, got):
    return pl.pallas_call(
        choose_kernel,
        out_shape=jax.ShapeDtypeStruct((2, CB * BLK, BLK), F32),
        in_specs=[SMEM, ANY, ANY],
        out_specs=VMEM,
        scratch_shapes=[pltpu.SemaphoreType.DMA((2,))],
        compiler_params=params(),
        cost_estimate=cost(0, 1 << 20),
    )(meta, keep, got)


def band_kernel(meta, keep, got, far, o0, o1, o2, o3, sems):
    r, s = meta[0], meta[1]
    k = lax.rem(s, 2)
    hi = lax.div(s, 2)
    outs = (o0, o1, o2, o3)
    for m in range(2):
        base = OWN + 24 * m
        j = place_of(meta, base, s)
        src = lax.div(jnp.maximum(j, 0), CB)
        near = lax.div(src, 2) == hi
        same = lax.rem(src, 2) == k
        options = (
            (near & same, keep.at[hi, m]),
            (near & jnp.logical_not(same), got.at[hi, m]),
            (jnp.logical_not(near), far.at[m]),
        )
        targets, ranks, _ = ranked(meta, base, r)
        for i in range(CB):
            shift = lax.rem(targets[i] - r + ROWS, ROWS)
            for take, ref in options:

                @pl.when(take)
                def _():
                    block = ref.at[pl.ds(i * BLK, BLK)]
                    for d in range(ROWS):

                        @pl.when(shift == d)
                        def _():
                            pltpu.make_async_copy(
                                block, outs[d].at[m * CAP + ranks[i]], sems.at[m * CB + i, 0]
                            ).start()

                    @pl.when(targets[i] == 0)
                    def _():
                        for d in range(ROWS):
                            pltpu.make_async_copy(
                                block, outs[d].at[4 + m * CAP + ranks[i]], sems.at[m * CB + i, 1 + d]
                            ).start()

        for i in range(CB):
            done = far.at[0, pl.ds(0, BLK)]
            pltpu.make_async_copy(done, o0.at[0], sems.at[m * CB + i, 0]).wait()

            @pl.when(targets[i] == 0)
            def _():
                for d in range(ROWS):
                    pltpu.make_async_copy(done, o0.at[0], sems.at[m * CB + i, 1 + d]).wait()


def band(meta, keep, got, far):
    shape = jax.ShapeDtypeStruct((4 * CAP, BLK, BLK), F32)
    return pl.pallas_call(
        band_kernel,
        out_shape=(shape,) * 4,
        in_specs=[SMEM] + [ANY] * 3,
        out_specs=(VMEM,) * 4,
        scratch_shapes=[pltpu.SemaphoreType.DMA((2 * CB, 1 + ROWS))],
        compiler_params=params(),
        cost_estimate=cost(0, 1 << 20),
    )(meta, keep, got, far)


def strip_kernel(meta, fs, fd, x0, x1, x2, x3, out):
    r, s = meta[0], meta[1]
    out[: PB * BLK, :] = fs[...]
    out[PB * BLK :, :] = fd[...]
    for m in range(2):
        base = OWN + 24 * m
        there = place_of(meta, base, s) >= 0
        for d, x in enumerate((x0, x1, x2, x3)):
            sender = lax.rem(r - d + ROWS, ROWS)
            targets, ranks, places = ranked(meta, base, sender)
            for i in range(CB):

                @pl.when(there & (targets[i] == r))
                def _():
                    rows = pl.ds(pl.multiple_of(places[i] * BLK, BLK), BLK)
                    out[rows, :] += x[m * CAP + ranks[i]]

                @pl.when(there & (targets[i] == 0) & (places[i] < 4))
                def _():
                    rows = pl.ds(pl.multiple_of((PB + places[i]) * BLK, BLK), BLK)
                    out[rows, :] += x[4 + m * CAP + ranks[i]]


def strip_add(meta, fs, fd, xs):
    return pl.pallas_call(
        strip_kernel,
        out_shape=jax.ShapeDtypeStruct(((PB + 4) * BLK, BLK), F32),
        in_specs=[SMEM] + [VMEM] * 6,
        out_specs=VMEM,
        compiler_params=params(),
        cost_estimate=cost(0, 1 << 20),
    )(meta, fs, fd, *xs)


def dot(a, b, dims=((1,), (0,))):
    return lax.dot_general(a, b, (dims, ((), ())), precision=HIGHEST, preferred_element_type=F32)


def dot_t(a, b):
    return dot(a, b, ((1,), (1,)))


def inverse_factor(block):
    groups = BLK // 8
    left = [block[8 * g : 8 * g + 8, :] for g in range(groups)]
    sub = lax.broadcasted_iota(jnp.int32, (8, BLK), 0)
    lane = lax.broadcasted_iota(jnp.int32, (8, BLK), 1)
    right = [(lane == sub + 8 * g).astype(F32) for g in range(groups)]
    for k in range(BLK):
        g0, kk = divmod(k, 8)
        row_l = left[g0][kk : kk + 1, :]
        row_r = right[g0][kk : kk + 1, :]
        inv = 1.0 / row_l[:, k : k + 1]
        row_l = row_l * inv
        row_r = row_r * inv
        for g in range(g0, groups):
            if g == g0 and kk == 7:
                continue
            col = left[g][:, k : k + 1]
            if g == g0:
                col = jnp.where(sub[:, :1] > kk, col, 0.0)
            left[g] = left[g] - col * row_l
            right[g] = right[g] - col * row_r
    out = []
    for g in range(groups):
        diag = jnp.sum(jnp.where(lane == sub + 8 * g, left[g], 0.0), axis=1, keepdims=True)
        out.append(right[g] / jnp.sqrt(diag))
    return jnp.concatenate(out, axis=0)


def pick(s, own, got, q, rows=slice(None)):
    far = jnp.not_equal(lax.div(s, 2), q // 2).astype(jnp.int32)
    return jnp.where(lax.rem(s, 2) == q % 2, own[far, rows], got[far, rows])


def inverse_panel(a, low, w, out):
    def step(b, carry):
        at = pl.ds(pl.multiple_of(b * BLK, BLK), BLK)
        w[b] = inverse_factor(a[at, at])

        @pl.when(b == 0)
        def _():
            below = dot_t(a[BLK:, :BLK], w[0])
            low[...] = below
            a[BLK:, BLK:] -= dot_t(below, below)

        return carry

    lax.fori_loop(0, 2, step, 0)
    out[:BLK, :BLK] = w[0]
    out[:BLK, BLK:] = jnp.zeros((BLK, BLK), F32)
    out[BLK:, :BLK] = -dot(dot(w[1], low[...]), w[0])
    out[BLK:, BLK:] = w[1]


def symmetric(d):
    return 0.5 * (d + d.T)


def first_kernel(meta, own, got, w0, l10, rest, tick, a, low, w):
    s = meta[1]
    d = jnp.concatenate([pick(s, own, got, q) for q in range(4)], axis=1)
    a[...] = symmetric(d[:PW, :PW])
    inverse_panel(a, low, w, w0)
    below = dot_t(d[PW:, :PW], w0[...])
    l10[...] = below
    rest[...] = symmetric(d[PW:, PW:] - dot_t(below, below))
    tick[...] = jnp.zeros_like(tick)


def second_kernel(rest, _, w1, tick, a, low, w):
    a[...] = rest[...]
    inverse_panel(a, low, w, w1)
    tick[...] = jnp.zeros_like(tick)


FACTOR_SCRATCH = [
    pltpu.VMEM((PW, PW), F32),
    pltpu.VMEM((BLK, BLK), F32),
    pltpu.VMEM((2, BLK, BLK), F32),
]


def factor_first(meta, own, got):
    shape = jax.ShapeDtypeStruct((PW, PW), F32)
    diag = pl.BlockSpec((2, 2 * PW, BLK), lambda i: (0, 3, 0))
    whole = pl.BlockSpec((PW, PW), lambda i: (0, 0))
    return pl.pallas_call(
        first_kernel,
        grid=(1,),
        out_shape=(shape, shape, shape, TICK),
        in_specs=[SMEM, diag, diag],
        out_specs=(whole, whole, whole, pl.BlockSpec((8, BLK), lambda i: (0, 0))),
        scratch_shapes=FACTOR_SCRATCH,
        compiler_params=params(),
        cost_estimate=cost(0, 90 << 20),
    )(meta, own, got)


def factor_second(rest, tick):
    return pl.pallas_call(
        second_kernel,
        out_shape=(jax.ShapeDtypeStruct((PW, PW), F32), TICK),
        in_specs=[VMEM, VMEM],
        out_specs=(VMEM, VMEM),
        scratch_shapes=FACTOR_SCRATCH,
        compiler_params=params(),
        cost_estimate=cost(0, 90 << 20),
    )(rest, tick)


def split(x):
    high = x.astype(jnp.bfloat16)
    return high, (x - high.astype(F32)).astype(jnp.bfloat16)


def solve(x, w0, l10, w1):
    first = dot_t(x[:, :PW], w0)
    second = dot_t(x[:, PW:] - dot_t(first, l10), w1)
    return first, second


def rows_kernel(meta, own, got, w0, l10, w1, _, low, high, rest):
    i = pl.program_id(0)
    x = jnp.concatenate([pick(meta[1], own, got, q) for q in range(4)], axis=1)
    first, second = solve(x, w0[...], l10[...], w1[...])
    second = jnp.where((i == 0) & (meta[0] == 0), 0.0, second)
    whole = jnp.concatenate([first, second], axis=1)
    low[...] = whole
    high[...], rest[...] = split(whole)


def factor_rows(meta, own, got, w0, l10, w1, tick):
    n = PB * BLK
    src = pl.BlockSpec((2, PW, BLK), lambda i: (0, i, 0))
    whole = pl.BlockSpec((PW, PW), lambda i: (0, 0))
    out = pl.BlockSpec((PW, 2 * PW), lambda i: (i, 0))
    return pl.pallas_call(
        rows_kernel,
        grid=(n // PW,),
        out_shape=(
            jax.ShapeDtypeStruct((n, 2 * PW), F32),
            jax.ShapeDtypeStruct((n, 2 * PW), jnp.bfloat16),
            jax.ShapeDtypeStruct((n, 2 * PW), jnp.bfloat16),
        ),
        in_specs=[SMEM, src, src, whole, whole, whole, pl.BlockSpec((8, BLK), lambda i: (0, 0))],
        out_specs=(out, out, out),
        compiler_params=params(),
        cost_estimate=cost(0, 1 << 20),
    )(meta, own, got, w0, l10, w1, tick)


def cols_kernel(meta, o0, g0, o1, g1, o2, g2, o3, g3, w0, l10, w1, high, rest):
    r, s = meta[0], meta[1]
    away = lax.rem(r - s + ROWS, ROWS)
    owns, gots = (o0, o1, o2, o3), (g0, g1, g2, g3)
    own, got = o0[...], g0[...]
    for d in range(1, ROWS):
        own = jnp.where(away == d, owns[d][...], own)
        got = jnp.where(away == d, gots[d][...], got)
    k = lax.rem(s, 2) == 0
    hi = lax.div(s, 2) == 0
    parts = []
    for q in range(4):
        mine, other = (own, got) if q % 2 == 0 else (got, own)
        both = jnp.where(k, mine, other)
        parts.append(jnp.where(hi, both[q // 2], both[1 - q // 2]))
    x = jnp.concatenate(parts, axis=1)
    first, second = solve(x, w0[...], l10[...], w1[...])
    whole = jnp.concatenate([first, second], axis=1).T
    high[...], rest[...] = split(whole)


def factor_cols(meta, pairs, w0, l10, w1):
    n = PB * BLK

    def src(d):
        return pl.BlockSpec(
            (2, PW, BLK),
            lambda i, meta: (0, jnp.where(lax.rem(meta[0] - meta[1] + ROWS, ROWS) == d, i, 0), 0),
        )

    whole = pl.BlockSpec((PW, PW), lambda i, meta: (0, 0))
    out = pl.BlockSpec((2 * PW, PW), lambda i, meta: (0, i))
    return pl.pallas_call(
        cols_kernel,
        grid_spec=pltpu.PrefetchScalarGridSpec(
            num_scalar_prefetch=1,
            grid=(n // PW,),
            in_specs=[src(d) for d in range(ROWS) for _ in range(2)] + [whole] * 3,
            out_specs=(out, out),
        ),
        out_shape=(jax.ShapeDtypeStruct((2 * PW, n), jnp.bfloat16),) * 2,
        compiler_params=params(),
        cost_estimate=cost(0, 1 << 20),
    )(meta, *[x for pair in pairs for x in pair], w0, l10, w1)


def table_kernel(meta, out):
    for n in range(6 * PB + 16):
        out[n] = jnp.int32(-1)
    for c in range(2):
        base = OWN + 24 * c
        for axis in range(2):
            here = meta[axis]
            for sender in range(ROWS):
                targets, ranks, places = ranked(meta, base, sender)
                for i in range(CB):

                    @pl.when(targets[i] == here)
                    def _():
                        out[(3 * c + axis) * PB + places[i]] = CAP * sender + ranks[i]
                        if c == 1 and axis == 0:
                            out[6 * PB + CAP * sender + ranks[i]] = places[i]

        last = jnp.int32(0)
        for p in range(PB):
            slot = out[3 * c * PB + p]
            last = jnp.where(slot >= 0, slot, last)
            out[(3 * c + 2) * PB + p] = last
    first = jnp.int32(0)
    for j in reversed(range(8)):
        first = jnp.where(out[6 * PB + j] >= 0, out[6 * PB + j], first)
    for j in range(8):
        at = out[6 * PB + j]
        out[6 * PB + 8 + j] = (at >= 0).astype(jnp.int32)
        first = jnp.where(at >= 0, at, first)
        out[6 * PB + j] = first


def tables(meta):
    return pl.pallas_call(
        table_kernel,
        out_shape=jax.ShapeDtypeStruct((6 * PB + 16,), jnp.int32),
        in_specs=[SMEM],
        out_specs=SMEM,
    )(meta)


def trail_kernel(meta, tab, front, xa, low, rh, rl, ch, cl, out):
    p = pl.program_id(0)
    r, s = meta[0], meta[1]
    top = (r == 0) & (p < 4)

    @pl.when(top)
    def _():
        out[...] = jnp.zeros_like(out)

    @pl.when(jnp.logical_not(top))
    def _():
        def mul(a, b):
            return lax.dot_general(a, b, (((1,), (0,)), ((), ())), preferred_element_type=F32)

        for c in range(PB * BLK // PW):
            at = slice(c * PW, (c + 1) * PW)
            prod = mul(rh[...], ch[:, at]) + (mul(rh[...], cl[:, at]) + mul(rl[...], ch[:, at]))
            out[:, at] = front[:, at] - prod
        there = tab[p] >= 0
        for q in range(PB):
            slot = tab[PB + q]

            @pl.when(there & (slot >= 0))
            def _():
                at = slice(q * BLK, (q + 1) * BLK)
                out[:, at] += xa[0, lax.div(slot, 2), 0, lax.rem(slot, 2)]

    @pl.when(s == 0)
    def _():
        out[:, : 2 * PW] = low[...]


def trail(meta, tab, front, xa, low, rh, rl, ch, cl):
    n = PB * BLK

    def index(p, meta, tab):
        slot = tab[2 * PB + p]
        return (lax.div(slot, 2), 0, lax.rem(slot, 2), 0, 0, 0)

    wide = pl.BlockSpec((BLK, n), lambda p, meta, tab: (p, 0))
    rows = pl.BlockSpec((BLK, 2 * PW), lambda p, meta, tab: (p, 0))
    cols = pl.BlockSpec((2 * PW, n), lambda p, meta, tab: (0, 0))
    return pl.pallas_call(
        trail_kernel,
        grid_spec=pltpu.PrefetchScalarGridSpec(
            num_scalar_prefetch=2,
            grid=(PB,),
            in_specs=[wide, pl.BlockSpec((1, 4, 1, 2, BLK, BLK), index)]
            + [rows, rows, rows, cols, cols],
            out_specs=wide,
        ),
        out_shape=jax.ShapeDtypeStruct((n, n), F32),
        compiler_params=params(),
        cost_estimate=cost(0, 1 << 20),
    )(meta, tab, front, xa, low, rh, rl, ch, cl)


def last_kernel(meta, tab, front, xb, out):
    j = pl.program_id(0)
    p = tab[6 * PB + j]
    fresh = (j == 0) | (p != tab[6 * PB + jnp.maximum(j - 1, 0)])

    @pl.when(fresh)
    def _():
        out[...] = front[...]

    add = (tab[6 * PB + 8 + j] > 0) & jnp.logical_not((meta[0] == 0) & (p < 4))
    for q in range(PB):
        slot = tab[4 * PB + q]

        @pl.when(add & (slot >= 0) & ((meta[1] > 0) | (q >= 4)))
        def _():
            at = slice(q * BLK, (q + 1) * BLK)
            out[:, at] += xb[0, lax.div(slot, 2), 0, lax.rem(slot, 2)]


def last(meta, tab, front, xb):
    n = PB * BLK
    wide = pl.BlockSpec((BLK, n), lambda j, meta, tab: (tab[6 * PB + j], 0))
    return pl.pallas_call(
        last_kernel,
        grid_spec=pltpu.PrefetchScalarGridSpec(
            num_scalar_prefetch=2,
            grid=(2 * ROWS,),
            in_specs=[
                wide,
                pl.BlockSpec(
                    (1, 4, 1, 2, BLK, BLK),
                    lambda j, meta, tab: (lax.div(j, 2), 0, lax.rem(j, 2), 0, 0, 0),
                ),
            ],
            out_specs=wide,
        ),
        out_shape=jax.ShapeDtypeStruct((n, n), F32),
        input_output_aliases={2: 0},
        compiler_params=params(),
        cost_estimate=cost(0, 1 << 20),
    )(meta, tab, front, xb)


def move(x, axes, fn, sizes, only=None):
    pairs = []
    total = 1
    for size in sizes:
        total *= size

    def unflat(i):
        place = []
        for size in reversed(sizes):
            place.append(i % size)
            i //= size
        return tuple(reversed(place))

    def flat(place):
        i = 0
        for at, size in zip(place, sizes):
            i = i * size + at
        return i

    for i in range(total):
        place = unflat(i)
        if only is None or only(*place):
            pairs.append((i, flat(fn(*place))))
    return lax.ppermute(x, axes if len(axes) > 1 else axes[0], pairs)


def across_cube(x):
    return move(x, ("cube",), lambda g: (g ^ 1,), (8,))


def across_col(x, mask):
    return move(x, ("col",), lambda s: (s ^ mask,), (4,))


def exchange(packed):
    per = packed.shape[0] // 16
    got = lax.all_to_all(packed.reshape(16, per, BLK, BLK), ("row", "col"), 0, 0, tiled=True)
    return got.reshape(4, 4, per // 2, 2, BLK, BLK)


def shards(front_entries, child_update, block_map):
    barrier = lax.optimization_barrier
    front = front_entries[0]
    child = child_update[0]
    row_here, col_here = lax.axis_index("row"), lax.axis_index("col")
    here = jnp.stack([row_here, col_here]).astype(jnp.int32)
    meta = jnp.concatenate([here, block_map.reshape(-1)])
    n = PB * BLK

    sibling = across_cube(child)

    fs = [front[:, q * BLK : (q + 1) * BLK] for q in range(4)]
    moved = [move(fs[q], ("col",), lambda s: (q,), (4,), lambda s: s == 0) for q in range(1, 4)]
    xa = exchange(pack(meta, child, OWN, meta))

    keep, send = strips(meta, child, sibling)
    got = across_col(send, 1)
    chosen = choose(meta, keep, got)
    far = across_col(chosen, 2)
    xa, far = barrier((xa, far))
    outs = band(meta, keep, got, far)
    moved, outs = barrier((moved, outs))
    fs = jnp.where(col_here == 0, fs[0], moved[0] + moved[1] + moved[2])
    top = fs[: 2 * PW]
    tops = [move(top, ("row",), lambda r: (d,), (4,), lambda r: r == 0) for d in range(1, 4)]
    fd = jnp.where(row_here == 0, top, tops[0] + tops[1] + tops[2])
    xs = [outs[0]] + [
        move(outs[d], ("row",), lambda r: ((r + d) % 4,), (4,)) for d in range(1, 4)
    ]
    mine = strip_add(meta, fs, fd, xs)

    own = jnp.stack([mine, across_col(mine, 2)])
    other = across_col(own, 1)
    tab = tables(meta)

    def step(x, start, stop):
        return move(
            x,
            ("row", "col"),
            lambda r, s: ((s + stop) % 4, s),
            (4, 4),
            lambda r, s: r == (s + start) % 4,
        )

    own_band, other_band = own[:, :n], other[:, :n]
    o1, o3 = step(own_band, 0, 1), step(own_band, 0, 3)
    g1, g3 = step(other_band, 0, 1), step(other_band, 0, 3)
    w0, l10, rest, tick = factor_first(meta, own, other)
    tick = across_col(tick, 1)
    o1, o3, g1, g3, rest, tick = barrier((o1, o3, g1, g3, rest, tick))
    o2, g2 = step(o1, 1, 2), step(g3, 3, 2)
    w1, tick = factor_second(rest, tick)
    tick = across_col(tick, 1)
    w0, l10, w1, tick, o2, g2, sibling = barrier((w0, l10, w1, tick, o2, g2, sibling))
    packed = pack(meta, sibling, OWN + 24, tick)
    packed, w1 = barrier((packed, w1))
    xb = exchange(packed)
    low, rh, rl = factor_rows(meta, own, other, w0, l10, w1, tick)
    ch, cl = factor_cols(
        meta, ((own, other), (o1, g1), (o2, g2), (o3, g3)), w0, l10, w1
    )
    whole = trail(meta, tab, front, xa, low, rh, rl, ch, cl)
    return last(meta, tab, whole, xb)[None]


def solution(mesh):
    in_specs = (P("cube", "row", "col"), P("cube", "row", "col"), P("cube", None, None))
    out_specs = P("cube", "row", "col")
    return jax.shard_map(shards, mesh=mesh, in_specs=in_specs, out_specs=out_specs, check_vma=False)
```

time: 892 us -> 313 us (0.35); the launches traced: 877 us -> 311 us
  waiting for transfers between devices: 413 us -> 108 us
  other arithmetic: 139 us -> 4.62 us
  Pallas kernels: 0 us -> 129 us
  local copies, waits for them, and re-layouts: 127 us -> 7.74 us
  blocking collectives: 93.3 us -> 0 us
  matrix products: 76.6 us -> 0 us
  starting transfers between devices: 11.1 us -> 62.1 us
  between operations: 16.7 us -> 0.28 us
    psum x6 -> x0, waiting for transfers between devices: 287 us -> none  [spread(): return lax.psum(jnp.where(mine, x, jnp.zeros_like(x)), axis)]
    pallas_call x0 -> x13, Pallas kernels: none -> 129 us  [the longest x1 25.8 us: factor_first(): pl.pallas_call(first_kernel, grid=(1,), out_shape=(shape, shape, shape, T...]
    another operation x21 -> x2, other arithmetic: 110 us -> 1.55 us  [shards(): own = jnp.stack([mine, across_col(mine, 2)])]
    all_to_all x1 -> x0, blocking collectives: 93.3 us -> none  [shards(): lax.all_to_all(packed, 'row', split_axis=1, concat_axis=1, tiled=True)]
    dot_general x10 -> x0, matrix products: 70.2 us -> none  [the longest x2 22.7 us: shards(): jnp.dot(trail_rows, trail_cols.T, precision=highest, preferred_element_ty...]
    all_to_all x1 -> x2, waiting for transfers between devices: 80.6 us -> 13 us  [exchange(): lax.all_to_all(packed.reshape(16, per, BLK, BLK), ('row', 'col'), 0, 0, t...]
    reshape x5 -> x1, local copies, waits for them, and re-layouts: 53.5 us -> 0.76 us  [shards(): meta = jnp.concatenate([here, block_map.reshape(-1)])]
    ppermute x1 -> x22, waiting for transfers between devices: 45 us -> 94.9 us  [move(): return lax.ppermute(x, axes if len(axes) > 1 else axes[0], pairs)]
  transfers between devices with their start and end apart: 8 -> 24, of which waited for: 8 -> 10; matrix products, arithmetic and copies ran while one was open for 2% -> 1% of each run, Pallas kernels for 0% -> 36%
where the time goes in v1:
time: 313 us; the launch traced here: 311 us
  Pallas kernels  129 us (41%)
  waiting for transfers between devices  108 us (35%)
  starting transfers between devices  62.1 us (20%)
  local copies, waits for them, and re-layouts  7.74 us (2%)
  other arithmetic  4.62 us (1%)
    ppermute x22, waiting for transfers between devices, move(): return lax.ppermute(x, axes if len(axes) > 1 else axes[0], pairs)  94.9 us
    ppermute x22, starting transfers between devices, move(): return lax.ppermute(x, axes if len(axes) > 1 else axes[0], pairs)  45.3 us
    pallas_call x1, Pallas kernels, factor_first(): pl.pallas_call(first_kernel, grid=(1,), out_shape=(shape, shape, shape, T...  25.8 us
    pallas_call x1, Pallas kernels, factor_second(): pl.pallas_call(second_kernel, out_shape=(jax.ShapeDtypeStruct((PW, PW), F...  24.3 us
    pallas_call x1, Pallas kernels, trail(): pl.pallas_call(trail_kernel, grid_spec=pltpu.PrefetchScalarGridSpec(num_s...  19.7 us
    all_to_all x2, starting transfers between devices, exchange(): lax.all_to_all(packed.reshape(16, per, BLK, BLK), ('row', 'col'), 0, 0, t...  16.8 us
    pallas_call x1, Pallas kernels, factor_cols(): pl.pallas_call(cols_kernel, grid_spec=pltpu.PrefetchScalarGridSpec(num_sc...  13.4 us
    all_to_all x2, waiting for transfers between devices, exchange(): lax.all_to_all(packed.reshape(16, per, BLK, BLK), ('row', 'col'), 0, 0, t...  13 us
  transfers between devices with their start and end apart: 24, of which 10 were waited for; matrix products, arithmetic and copies ran while one was open for 1% of the time, Pallas kernels for 36%

profile of v1, /device:TPU:85, one launch (start us, length us, event | category | flops | bytes accessed | tf_op | source)
XLA Modules:
  0.0 311.2 jit_solution(9344571222441771745)
XLA Ops:
  2.7 3.4 %shard_map.38 = f32[64,128,128]{2,1,0:T(8,128)} custom-call(s32[50]{0:T(128)} %pad_add_fusion.meta._, f32[768,768]{1,0:T(8,128)} %bitcast.19, s32[50]{0:T(128)} %pad_add_fusion.meta._), custom_call_target="tpu_custom_call" | custom-call | bytes 1048576 | tf_op jit(solution)/shard_map/pallas_call | solution.py:72
  6.0 7.8 %all-to-all-start = ((f32[16,4,128,128]{3,2,1,0:T(8,128)}), f32[16,4,128,128]{3,2,1,0:T(8,128)}, u32[]{:S(2)}, u32[]{:S(2)}) async-start(f32[16,4,128,128]{3,2,1,0:T(8,128)} %bitcast.14), calls=%async_computation | async-start | bytes 8388608 | tf_op jit(solution)/shard_map/all_to_all | solution.py:627
  13.9 38.6 %collective-permute-done.sibling.child = f32[768,768]{1,0:T(8,128)S(1)} collective-permute-done((f32[768,768]{1,0:T(8,128)}, f32[768,768]{1,0:T(8,128)S(1)}, u32[]{:S(2)}, u32[]{:S(2)}) %collective-permute-start) | collective-permute-done | bytes 2359328 | tf_op jit(solution)/shard_map/ppermute | solution.py:614
  53.9 4.2 %shard_map.39 = (f32[2,2,768,128]{3,2,1,0:T(8,128)}, f32[2,2,768,128]{3,2,1,0:T(8,128)}) custom-call(s32[50]{0:T(128)} %pad_add_fusion.meta._, f32[768,768]{1,0:T(8,128)} %bitcast.20, f32[768,768]{1,0:T(8,128)} %copy-done.3), custom_call_target="tpu_custom_call" | custom-call | bytes 1048576 | tf_op jit(solution)/shard_map/pallas_call | solution.py:107
  59.6 3.2 %collective-permute-done.1.got = f32[2,2,768,128]{3,2,1,0:T(8,128)S(1)} collective-permute-done((f32[2,2,768,128]{3,2,1,0:T(8,128)}, f32[2,2,768,128]{3,2,1,0:T(8,128)S(1)}, u32[]{:S(2)}, u32[]{:S(2)}) %collective-permute-start.1) | collective-permute-done | bytes 1572896 | tf_op jit(solution)/shard_map/ppermute | solution.py:614
  64.1 2.8 shard_map.40
  67.0 1.8 fusion.1
  70.1 1.5 collective-permute-start.4
  71.6 1.5 collective-permute-start.3
  73.2 16.4 %collective-permute-done.2.far = f32[2,768,128]{2,1,0:T(8,128)} collective-permute-done((f32[2,768,128]{2,1,0:T(8,128)}, f32[2,768,128]{2,1,0:T(8,128)}, u32[]{:S(2)}, u32[]{:S(2)}) %collective-permute-start.2) | collective-permute-done | bytes 786464 | tf_op jit(solution)/shard_map/ppermute | solution.py:614
  89.5 4.9 %shard_map.41 = (f32[8,128,128]{2,1,0:T(8,128)}, f32[8,128,128]{2,1,0:T(8,128)}, f32[8,128,128]{2,1,0:T(8,128)}, f32[8,128,128]{2,1,0:T(8,128)}) custom-call(s32[50]{0:T(128)} %pad_add_fusion.meta._, f32[2,2,768,128]{3,2,1,0:T(8,128)} %get-tuple-element.46.keep, f32[2,2,768,128]{3,2,1,0:T(8,128)} %copy-done.4, f32[2,768,128]{2,1,0:T(8,128)} %collective-permute-done.2.far), custom_call_target="tpu_custom_call" | custom-call | bytes 1048576 | tf_op jit(solution)/shard_map/pallas_call | solution.py:201
  94.4 3.2 %collective-permute-done.5 = f32[1536,128]{1,0:T(8,128)S(1)} collective-permute-done((f32[1536,128]{1,0:T(8,128)S(1)}, f32[1536,128]{1,0:T(8,128)S(1)}, u32[]{:S(2)}, u32[]{:S(2)}) %collective-permute-start.5) | collective-permute-done | bytes 786464 | tf_op jit(solution)/shard_map/ppermute | solution.py:614
  97.7 1.8 slice_select_fusion.fs
  100.4 2.5 collective-permute-start.10
  102.9 2.0 collective-permute-start.11
  106.9 15.4 %collective-permute-done.7 = f32[512,128]{1,0:T(8,128)S(1)} collective-permute-done((f32[512,128]{1,0:T(8,128)S(1)}, f32[512,128]{1,0:T(8,128)S(1)}, u32[]{:S(2)}, u32[]{:S(2)}) %collective-permute-start.7) | collective-permute-done | bytes 262176 | tf_op jit(solution)/shard_map/ppermute | solution.py:614
  125.0 3.8 %shard_map.42 = f32[2048,128]{1,0:T(8,128)} custom-call(s32[50]{0:T(128)} %pad_add_fusion.meta._, f32[1536,128]{1,0:T(8,128)} %copy-done.5, f32[512,128]{1,0:T(8,128)} %add_select_fusion.fd, f32[8,128,128]{2,1,0:T(8,128)} %get-tuple-element.57.x0, f32[8,128,128]{2,1,0:T(8,128)} %copy-done.9, f32[8,128,128]{2,1,0:T(8,128)} %copy-done.10, ...), custom_call_target="tpu_custom_call" | custom-call | bytes 1048576 | tf_op jit(solution)/shard_map/pallas_call | solution.py:236
  128.8 15.4 %collective-permute-done.12 = f32[2048,128]{1,0:T(8,128)S(1)} collective-permute-done((f32[2048,128]{1,0:T(8,128)}, f32[2048,128]{1,0:T(8,128)S(1)}, u32[]{:S(2)}, u32[]{:S(2)}) %collective-permute-start.12) | collective-permute-done | bytes 1048608 | tf_op jit(solution)/shard_map/ppermute | solution.py:614
  145.6 14.4 %collective-permute-start.13 = (f32[2,2048,128]{2,1,0:T(8,128)S(1)}, f32[2,2048,128]{2,1,0:T(8,128)S(1)}, u32[]{:S(2)}, u32[]{:S(2)}) collective-permute-start(f32[2,2048,128]{2,1,0:T(8,128)S(1)} %pad_maximum_fusion.own.o0), channel_id=1, source_target_pairs={{0,1},{1,0},{2,3},{3,2},{4,5},{5,4},{6,7},{7,6},{8,9},{9,8},{10,11... | collective-permute-start | bytes 6291464 | tf_op jit(solution)/shard_map/ppermute | solution.py:614
  161.5 1.8 collective-permute-start.14
  165.2 1.8 collective-permute-start.16
  167.1 25.8 %shard_map.43 = (f32[256,256]{1,0:T(8,128)}, f32[256,256]{1,0:T(8,128)}, f32[256,256]{1,0:T(8,128)}, f32[8,128]{1,0:T(8,128)}) custom-call(s32[50]{0:T(128)} %pad_add_fusion.meta._, f32[2,2048,128]{2,1,0:T(8,128)} %copy-done, f32[2,2048,128]{2,1,0:T(8,128)} %copy-done.1), custom_call_target="tpu_custom_call" | custom-call | bytes 94371840 | tf_op jit(solution)/shard_map/pallas_call | solution.py:339
  192.9 6.8 %collective-permute-start.18 = (f32[8,128]{1,0:T(8,128)}, f32[8,128]{1,0:T(8,128)S(1)}, u32[]{:S(2)}, u32[]{:S(2)}) collective-permute-start(f32[8,128]{1,0:T(8,128)} %get-tuple-element.64), channel_id=1, source_target_pairs={{0,1},{1,0},{2,3},{3,2},{4,5},{5,4},{6,7},{7,6},{8,9},{9,8},{10,11... | collective-permute-start | bytes 12296 | tf_op jit(solution)/shard_map/ppermute | solution.py:614
  202.9 24.3 %shard_map.44 = (f32[256,256]{1,0:T(8,128)}, f32[8,128]{1,0:T(8,128)}) custom-call(f32[256,256]{1,0:T(8,128)} %get-tuple-element.65.rest, f32[8,128]{1,0:T(8,128)} %copy-done.13), custom_call_target="tpu_custom_call" | custom-call | bytes 94371840 | tf_op jit(solution)/shard_map/pallas_call | solution.py:352
  229.7 4.0 %shard_map.45 = f32[64,128,128]{2,1,0:T(8,128)} custom-call(s32[50]{0:T(128)} %pad_add_fusion.meta._, f32[768,768]{1,0:T(8,128)} %copy-done.3, f32[8,128]{1,0:T(8,128)} %copy-done.12), custom_call_target="tpu_custom_call" | custom-call | bytes 1048576 | tf_op jit(solution)/shard_map/pallas_call | solution.py:72
  233.8 8.9 %all-to-all-start.1 = ((f32[16,4,128,128]{3,2,1,0:T(8,128)}), f32[16,4,128,128]{3,2,1,0:T(8,128)}, u32[]{:S(2)}, u32[]{:S(2)}) async-start(f32[16,4,128,128]{3,2,1,0:T(8,128)} %bitcast.15), calls=%async_computation.1 | async-start | bytes 8388608 | tf_op jit(solution)/shard_map/all_to_all | solution.py:627
  242.7 1.8 shard_map.37.tab
  244.5 10.8 %shard_map.46 = (f32[1536,512]{1,0:T(8,128)}, bf16[1536,512]{1,0:T(8,128)(2,1)}, bf16[1536,512]{1,0:T(8,128)(2,1)}) custom-call(s32[50]{0:T(128)} %pad_add_fusion.meta._, f32[2,2048,128]{2,1,0:T(8,128)} %copy-done, f32[2,2048,128]{2,1,0:T(8,128)} %copy-done.1, f32[256,256]{1,0:T(8,128)} %get-tuple-element.71.w0, f32[256,256]{1,0:T(8,128)} %get-tuple-element.72.l10, ...), custom_call_target="tpu_custom_call" | custom-call | bytes 1048576 | tf_op jit(solution)/shard_map/pallas_call | solution.py:389
  255.3 13.4 %shard_map.47 = (bf16[512,1536]{1,0:T(8,128)(2,1)}, bf16[512,1536]{1,0:T(8,128)(2,1)}) custom-call(s32[50]{0:T(128)} %pad_add_fusion.meta._, f32[2,2048,128]{2,1,0:T(8,128)} %copy-done, f32[2,2048,128]{2,1,0:T(8,128)} %copy-done.1, f32[2,1536,128]{2,1,0:T(8,128)} %collective-permute-done.14.o1, f32[2,1536,128]{2,1,0:T(8,128)} %collective-permute-done.16.g1, ...), custom_call_target="tpu_custom_call" | custom-call | bytes 1048576 | tf_op jit(solution)/shard_map/pallas_call | solution.py:436
  268.7 19.7 %shard_map.48.front = f32[1536,1536]{1,0:T(8,128)} custom-call(s32[50]{0:T(128)} %pad_add_fusion.meta._, s32[88]{0:T(128)} %shard_map.37.tab, f32[1536,1536]{1,0:T(8,128)} %bitcast.13, f32[4,4,2,2,128,128]{5,4,3,2,1,0:T(8,128)} %bitcast.5.xa, f32[1536,512]{1,0:T(8,128)} %get-tuple-element.77.low, bf16[1536,512]{1,0:T(8,128)(2,1)} %get-tuple-element.78.rh, ...), custom_call_target="tpu_custom_call" | custom-call | bytes 1048576 | tf_op jit(solution)/shard_map/pallas_call | solution.py:533
  288.3 13.0 %all-to-all-done.1 = f32[16,4,128,128]{3,2,1,0:T(8,128)} async-done(((f32[16,4,128,128]{3,2,1,0:T(8,128)}), f32[16,4,128,128]{3,2,1,0:T(8,128)}, u32[]{:S(2)}, u32[]{:S(2)}) %all-to-all-start.1) | async-done | bytes 4194336 | tf_op jit(solution)/shard_map/all_to_all | solution.py:627
  301.3 9.9 %shard_map.49 = f32[1536,1536]{1,0:T(8,128)} custom-call(s32[50]{0:T(128)} %pad_add_fusion.meta._, s32[88]{0:T(128)} %shard_map.37.tab, f32[1536,1536]{1,0:T(8,128)} %shard_map.48.front, f32[4,4,2,2,128,128]{5,4,3,2,1,0:T(8,128)} %bitcast.9.xb), custom_call_target="tpu_custom_call", output_to_operand_aliasing={{}: (2, {})} | custom-call | bytes 1048576 | tf_op jit(solution)/shard_map/pallas_call | solution.py:570
  (66 shorter events, 24.3 us)
Async XLA Ops:
  0.0 52.4 %collective-permute-start = (f32[768,768]{1,0:T(8,128)}, f32[768,768]{1,0:T(8,128)S(1)}, u32[]{:S(2)}, u32[]{:S(2)}) collective-permute-start(f32[768,768]{1,0:T(8,128)} %bitcast.18), channel_id=1, source_target_pairs={{0,16},{16,0},{32,48},{48,32},{64,80},{80,64},{96,112},{112,96},{1... | collective-permute-start | bytes 7077896 | tf_op jit(solution)/shard_map/ppermute | solution.py:614
  6.0 67.1 %all-to-all-start = ((f32[16,4,128,128]{3,2,1,0:T(8,128)}), f32[16,4,128,128]{3,2,1,0:T(8,128)}, u32[]{:S(2)}, u32[]{:S(2)}) async-start(f32[16,4,128,128]{3,2,1,0:T(8,128)} %bitcast.14), calls=%async_computation | async-start | bytes 8388608 | tf_op jit(solution)/shard_map/all_to_all | solution.py:627
  58.1 4.8 %collective-permute-start.1 = (f32[2,2,768,128]{3,2,1,0:T(8,128)}, f32[2,2,768,128]{3,2,1,0:T(8,128)S(1)}, u32[]{:S(2)}, u32[]{:S(2)}) collective-permute-start(f32[2,2,768,128]{3,2,1,0:T(8,128)} %get-tuple-element.47), channel_id=1, source_target_pairs={{0,1},{1,0},{2,3},{3,2},{4,5},{5,4},{6,7},{7,6},{8,9},{9,8},{10,11... | collective-permute-start | bytes 4718600 | tf_op jit(solution)/shard_map/ppermute | solution.py:614
  66.9 22.7 %collective-permute-start.2 = (f32[2,768,128]{2,1,0:T(8,128)}, f32[2,768,128]{2,1,0:T(8,128)}, u32[]{:S(2)}, u32[]{:S(2)}) collective-permute-start(f32[2,768,128]{2,1,0:T(8,128)} %shard_map.40), channel_id=1, source_target_pairs={{0,2},{1,3},{2,0},{3,1},{4,6},{5,7},{6,4},{7,5},{8,10},{9,11},{10,... | collective-permute-start | bytes 2359304 | tf_op jit(solution)/shard_map/ppermute | solution.py:614
  68.8 28.9 %collective-permute-start.5 = (f32[1536,128]{1,0:T(8,128)S(1)}, f32[1536,128]{1,0:T(8,128)S(1)}, u32[]{:S(2)}, u32[]{:S(2)}) collective-permute-start(f32[1536,128]{1,0:T(8,128)S(1)} %get-tuple-element.87), channel_id=1, source_target_pairs={{0,3},{4,7},{8,11},{12,15},{16,19},{20,23},{24,27},{28,31},{32,35}... | collective-permute-start | bytes 2359304 | tf_op jit(solution)/shard_map/ppermute | solution.py:614
  70.1 27.6 %collective-permute-start.4 = (f32[1536,128]{1,0:T(8,128)S(1)}, f32[1536,128]{1,0:T(8,128)}, u32[]{:S(2)}, u32[]{:S(2)}) collective-permute-start(f32[1536,128]{1,0:T(8,128)S(1)} %get-tuple-element.88), channel_id=1, source_target_pairs={{0,2},{4,6},{8,10},{12,14},{16,18},{20,22},{24,26},{28,30},{32,34}... | collective-permute-start | bytes 2359304 | tf_op jit(solution)/shard_map/ppermute | solution.py:614
  71.6 26.0 %collective-permute-start.3 = (f32[1536,128]{1,0:T(8,128)S(1)}, f32[1536,128]{1,0:T(8,128)}, u32[]{:S(2)}, u32[]{:S(2)}) collective-permute-start(f32[1536,128]{1,0:T(8,128)S(1)} %get-tuple-element.89), channel_id=1, source_target_pairs={{0,1},{4,5},{8,9},{12,13},{16,17},{20,21},{24,25},{28,29},{32,33},... | collective-permute-start | bytes 2359304 | tf_op jit(solution)/shard_map/ppermute | solution.py:614
  99.4 23.7 %copy-start.5 = (f32[1536,128]{1,0:T(8,128)}, f32[1536,128]{1,0:T(8,128)S(1)}, u32[]{:S(2)}) copy-start(f32[1536,128]{1,0:T(8,128)S(1)} %slice_select_fusion.fs) | copy-start | bytes 2359300
  99.5 6.8 %collective-permute-start.8 = (f32[512,128]{1,0:T(8,128)S(1)}, f32[512,128]{1,0:T(8,128)S(1)}, u32[]{:S(2)}, u32[]{:S(2)}) collective-permute-start(f32[512,128]{1,0:T(8,128)S(1)} %slice.32), channel_id=1, source_target_pairs={{0,12},{1,13},{2,14},{3,15},{16,28},{17,29},{18,30},{19,31},{32,44... | collective-permute-start | bytes 786440 | tf_op jit(solution)/shard_map/ppermute | solution.py:614
  100.2 23.0 %collective-permute-start.9 = (f32[8,128,128]{2,1,0:T(8,128)}, f32[8,128,128]{2,1,0:T(8,128)S(1)}, u32[]{:S(2)}, u32[]{:S(2)}) collective-permute-start(f32[8,128,128]{2,1,0:T(8,128)} %get-tuple-element.58), channel_id=1, source_target_pairs={{0,4},{4,8},{8,12},{12,0},{1,5},{5,9},{9,13},{13,1},{2,6},{6,10},{... | collective-permute-start | bytes 1572872 | tf_op jit(solution)/shard_map/ppermute | solution.py:614
  100.4 22.7 %collective-permute-start.10 = (f32[8,128,128]{2,1,0:T(8,128)}, f32[8,128,128]{2,1,0:T(8,128)S(1)}, u32[]{:S(2)}, u32[]{:S(2)}) collective-permute-start(f32[8,128,128]{2,1,0:T(8,128)} %get-tuple-element.59), channel_id=1, source_target_pairs={{0,8},{4,12},{8,0},{12,4},{1,9},{5,13},{9,1},{13,5},{2,10},{6,14},... | collective-permute-start | bytes 1572872 | tf_op jit(solution)/shard_map/ppermute | solution.py:614
  102.9 20.2 %collective-permute-start.11 = (f32[8,128,128]{2,1,0:T(8,128)}, f32[8,128,128]{2,1,0:T(8,128)S(1)}, u32[]{:S(2)}, u32[]{:S(2)}) collective-permute-start(f32[8,128,128]{2,1,0:T(8,128)} %get-tuple-element.60), channel_id=1, source_target_pairs={{0,12},{4,0},{8,4},{12,8},{1,13},{5,1},{9,5},{13,9},{2,14},{6,2},{... | collective-permute-start | bytes 1572872 | tf_op jit(solution)/shard_map/ppermute | solution.py:614
  104.9 17.4 %collective-permute-start.7 = (f32[512,128]{1,0:T(8,128)S(1)}, f32[512,128]{1,0:T(8,128)S(1)}, u32[]{:S(2)}, u32[]{:S(2)}) collective-permute-start(f32[512,128]{1,0:T(8,128)S(1)} %slice.32), channel_id=1, source_target_pairs={{0,8},{1,9},{2,10},{3,11},{16,24},{17,25},{18,26},{19,27},{32,40},... | collective-permute-start | bytes 786440 | tf_op jit(solution)/shard_map/ppermute | solution.py:614
  106.2 16.1 %collective-permute-start.6 = (f32[512,128]{1,0:T(8,128)S(1)}, f32[512,128]{1,0:T(8,128)S(1)}, u32[]{:S(2)}, u32[]{:S(2)}) collective-permute-start(f32[512,128]{1,0:T(8,128)S(1)} %slice.32), channel_id=1, source_target_pairs={{0,4},{1,5},{2,6},{3,7},{16,20},{17,21},{18,22},{19,23},{32,36},{3... | collective-permute-start | bytes 786440 | tf_op jit(solution)/shard_map/ppermute | solution.py:614
  128.8 15.4 %collective-permute-start.12 = (f32[2048,128]{1,0:T(8,128)}, f32[2048,128]{1,0:T(8,128)S(1)}, u32[]{:S(2)}, u32[]{:S(2)}) collective-permute-start(f32[2048,128]{1,0:T(8,128)} %shard_map.42), channel_id=1, source_target_pairs={{0,2},{1,3},{2,0},{3,1},{4,6},{5,7},{6,4},{7,5},{8,10},{9,11},{10,... | collective-permute-start | bytes 3145736 | tf_op jit(solution)/shard_map/ppermute | solution.py:614
  144.2 15.9 %copy-start.2 = (f32[2048,128]{1,0:T(8,128)S(1)}, f32[2048,128]{1,0:T(8,128)}, u32[]{:S(2)}) copy-start(f32[2048,128]{1,0:T(8,128)} %shard_map.42) | copy-start | bytes 3145732
  145.6 18.3 %copy-start = (f32[2,2048,128]{2,1,0:T(8,128)}, f32[2,2048,128]{2,1,0:T(8,128)S(1)}, u32[]{:S(2)}) copy-start(f32[2,2048,128]{2,1,0:T(8,128)S(1)} %pad_maximum_fusion.own.o0) | copy-start | bytes 6291460
  145.6 18.2 %collective-permute-start.13 = (f32[2,2048,128]{2,1,0:T(8,128)S(1)}, f32[2,2048,128]{2,1,0:T(8,128)S(1)}, u32[]{:S(2)}, u32[]{:S(2)}) collective-permute-start(f32[2,2048,128]{2,1,0:T(8,128)S(1)} %pad_maximum_fusion.own.o0), channel_id=1, source_target_pairs={{0,1},{1,0},{2,3},{3,2},{4,5},{5,4},{6,7},{7,6},{8,9},{9,8},{10,11... | collective-permute-start | bytes 6291464 | tf_op jit(solution)/shard_map/ppermute | solution.py:614
  160.2 39.6 %collective-permute-start.15 = (f32[2,1536,128]{2,1,0:T(8,128)S(1)}, f32[2,1536,128]{2,1,0:T(8,128)S(1)}, u32[]{:S(2)}, u32[]{:S(2)}) collective-permute-start(f32[2,1536,128]{2,1,0:T(8,128)S(1)} %fusion), channel_id=1, source_target_pairs={{0,12},{5,1},{10,6},{15,11},{16,28},{21,17},{26,22},{31,27},{32,44... | collective-permute-start | bytes 4718600 | tf_op jit(solution)/shard_map/ppermute | solution.py:614
  161.5 38.3 %collective-permute-start.14 = (f32[2,1536,128]{2,1,0:T(8,128)S(1)}, f32[2,1536,128]{2,1,0:T(8,128)}, u32[]{:S(2)}, u32[]{:S(2)}) collective-permute-start(f32[2,1536,128]{2,1,0:T(8,128)S(1)} %fusion), channel_id=1, source_target_pairs={{0,4},{5,9},{10,14},{15,3},{16,20},{21,25},{26,30},{31,19},{32,36}... | collective-permute-start | bytes 4718600 | tf_op jit(solution)/shard_map/ppermute | solution.py:614
  163.8 3.2 %copy-start.1 = (f32[2,2048,128]{2,1,0:T(8,128)}, f32[2,2048,128]{2,1,0:T(8,128)S(1)}, u32[]{:S(2)}) copy-start(f32[2,2048,128]{2,1,0:T(8,128)S(1)} %collective-permute-done.13.got.g0) | copy-start | bytes 6291460
  163.9 36.8 %collective-permute-start.17 = (f32[2,1536,128]{2,1,0:T(8,128)S(1)}, f32[2,1536,128]{2,1,0:T(8,128)}, u32[]{:S(2)}, u32[]{:S(2)}) collective-permute-start(f32[2,1536,128]{2,1,0:T(8,128)S(1)} %slice.35), channel_id=1, source_target_pairs={{0,12},{5,1},{10,6},{15,11},{16,28},{21,17},{26,22},{31,27},{32,44... | collective-permute-start | bytes 4718600 | tf_op jit(solution)/shard_map/ppermute | solution.py:614
  165.2 35.5 %collective-permute-start.16 = (f32[2,1536,128]{2,1,0:T(8,128)S(1)}, f32[2,1536,128]{2,1,0:T(8,128)}, u32[]{:S(2)}, u32[]{:S(2)}) collective-permute-start(f32[2,1536,128]{2,1,0:T(8,128)S(1)} %slice.35), channel_id=1, source_target_pairs={{0,4},{5,9},{10,14},{15,3},{16,20},{21,25},{26,30},{31,19},{32,36}... | collective-permute-start | bytes 4718600 | tf_op jit(solution)/shard_map/ppermute | solution.py:614
  192.9 7.9 %collective-permute-start.18 = (f32[8,128]{1,0:T(8,128)}, f32[8,128]{1,0:T(8,128)S(1)}, u32[]{:S(2)}, u32[]{:S(2)}) collective-permute-start(f32[8,128]{1,0:T(8,128)} %get-tuple-element.64), channel_id=1, source_target_pairs={{0,1},{1,0},{2,3},{3,2},{4,5},{5,4},{6,7},{7,6},{8,9},{9,8},{10,11... | collective-permute-start | bytes 12296 | tf_op jit(solution)/shard_map/ppermute | solution.py:614
  199.7 34.0 %copy-start.6 = (f32[2,1536,128]{2,1,0:T(8,128)}, f32[2,1536,128]{2,1,0:T(8,128)S(1)}, u32[]{:S(2)}) copy-start(f32[2,1536,128]{2,1,0:T(8,128)S(1)} %collective-permute-done.15.o3) | copy-start | bytes 4718596
  200.8 2.2 copy-start.13
  200.8 28.4 %collective-permute-start.20 = (f32[2,1536,128]{2,1,0:T(8,128)}, f32[2,1536,128]{2,1,0:T(8,128)S(1)}, u32[]{:S(2)}, u32[]{:S(2)}) collective-permute-start(f32[2,1536,128]{2,1,0:T(8,128)} %collective-permute-done.14.o1), channel_id=1, source_target_pairs={{3,7},{4,8},{9,13},{14,2},{19,23},{20,24},{25,29},{30,18},{35,39},... | collective-permute-start | bytes 4718600 | tf_op jit(solution)/shard_map/ppermute | solution.py:614
  201.5 27.6 %collective-permute-start.21 = (f32[2,1536,128]{2,1,0:T(8,128)}, f32[2,1536,128]{2,1,0:T(8,128)S(1)}, u32[]{:S(2)}, u32[]{:S(2)}) collective-permute-start(f32[2,1536,128]{2,1,0:T(8,128)} %collective-permute-done.17.g3), channel_id=1, source_target_pairs={{1,13},{6,2},{11,7},{12,8},{17,29},{22,18},{27,23},{28,24},{33,45}... | collective-permute-start | bytes 4718600 | tf_op jit(solution)/shard_map/ppermute | solution.py:614
  227.2 1.9 collective-permute-start.19
  229.1 4.6 %copy-start.7 = (f32[2,1536,128]{2,1,0:T(8,128)}, f32[2,1536,128]{2,1,0:T(8,128)S(1)}, u32[]{:S(2)}) copy-start(f32[2,1536,128]{2,1,0:T(8,128)S(1)} %collective-permute-done.20.o2) | copy-start | bytes 4718596
  229.2 4.6 %copy-start.8 = (f32[2,1536,128]{2,1,0:T(8,128)}, f32[2,1536,128]{2,1,0:T(8,128)S(1)}, u32[]{:S(2)}) copy-start(f32[2,1536,128]{2,1,0:T(8,128)S(1)} %collective-permute-done.21.g2) | copy-start | bytes 4718596
  233.8 67.5 %all-to-all-start.1 = ((f32[16,4,128,128]{3,2,1,0:T(8,128)}), f32[16,4,128,128]{3,2,1,0:T(8,128)}, u32[]{:S(2)}, u32[]{:S(2)}) async-start(f32[16,4,128,128]{3,2,1,0:T(8,128)} %bitcast.15), calls=%async_computation.1 | async-start | bytes 8388608 | tf_op jit(solution)/shard_map/all_to_all | solution.py:627
  (6 other events, 5.9 us)

commit v2 on v1

--- a/solution.py
+++ b/solution.py
@@ -78,6 +78,73 @@
         compiler_params=params(),
         cost_estimate=cost(0, 1 << 20),
     )(meta, child, tick)
+
+
+def row_pack_kernel(base, meta, child, o0, o1, o2, o3, sems):
+    outs = (o0, o1, o2, o3)
+    r = meta[0]
+    targets, ranks, _ = ranked(meta, base, r)
+    for i in range(CB):
+        shift = lax.rem(targets[i] - r + ROWS, ROWS)
+        for d in range(ROWS):
+
+            @pl.when(shift == d)
+            def _():
+                pltpu.make_async_copy(
+                    child.at[pl.ds(i * BLK, BLK)], outs[d].at[ranks[i]], sems.at[i]
+                ).start()
+
+    for i in range(CB):
+        pltpu.make_async_copy(child.at[pl.ds(0, BLK)], o0.at[0], sems.at[i]).wait()
+
+
+def row_pack(meta, child, base):
+    shape = jax.ShapeDtypeStruct((CAP, BLK, CB * BLK), F32)
+    return pl.pallas_call(
+        functools.partial(row_pack_kernel, base),
+        out_shape=(shape,) * 4,
+        in_specs=[SMEM, VMEM],
+        out_specs=(ANY,) * 4,
+        scratch_shapes=[pltpu.SemaphoreType.DMA((CB,))],
+        compiler_params=params(),
+        cost_estimate=cost(0, 1 << 20),
+    )(meta, child)
+
+
+def col_pack_kernel(base, meta, x0, x1, x2, x3, o0, o1, o2, o3, sems):
+    outs = (o0, o1, o2, o3)
+    s = meta[1]
+    targets, ranks, _ = ranked(meta, base, s)
+    for j in range(CB):
+        mask = jnp.bitwise_xor(targets[j], s)
+        for m in range(ROWS):
+
+            @pl.when(mask == m)
+            def _():
+                for d, x in enumerate((x0, x1, x2, x3)):
+                    for k in range(CAP):
+                        pltpu.make_async_copy(
+                            x.at[k, :, pl.ds(j * BLK, BLK)],
+                            outs[m].at[d * CAP + k, ranks[j]],
+                            sems.at[j, d * CAP + k],
+                        ).start()
+
+    for j in range(CB):
+        for n in range(2 * ROWS):
+            pltpu.make_async_copy(x0.at[0, :, pl.ds(0, BLK)], o0.at[0, 0], sems.at[j, n]).wait()
+
+
+def col_pack(meta, xs, base):
+    shape = jax.ShapeDtypeStruct((2 * ROWS, CAP, BLK, BLK), F32)
+    return pl.pallas_call(
+        functools.partial(col_pack_kernel, base),
+        out_shape=(shape,) * 4,
+        in_specs=[SMEM] + [VMEM] * 4,
+        out_specs=(ANY,) * 4,
+        scratch_shapes=[pltpu.SemaphoreType.DMA((CB, 2 * ROWS))],
+        compiler_params=params(),
+        cost_estimate=cost(0, 1 << 20),
+    )(meta, *xs)
 
 
 def strips_kernel(meta, child, sibling, keep, send, sems):
@@ -209,10 +276,15 @@
     )(meta, keep, got, far)
 
 
-def strip_kernel(meta, fs, fd, x0, x1, x2, x3, out):
+def strip_kernel(meta, f0, f1, f2, f3, x0, x1, x2, x3, out, sem):
     r, s = meta[0], meta[1]
-    out[: PB * BLK, :] = fs[...]
-    out[PB * BLK :, :] = fd[...]
+    for n, f in enumerate((f0, f1, f2, f3)):
+
+        @pl.when(s == n)
+        def _():
+            pltpu.make_async_copy(f, out, sem).start()
+
+    pltpu.make_async_copy(f0, out, sem).wait()
     for m in range(2):
         base = OWN + 24 * m
         there = place_of(meta, base, s) >= 0
@@ -232,15 +304,16 @@
                     out[rows, :] += x[4 + m * CAP + ranks[i]]
 
 
-def strip_add(meta, fs, fd, xs):
+def strip_add(meta, fs, xs):
     return pl.pallas_call(
         strip_kernel,
         out_shape=jax.ShapeDtypeStruct(((PB + 4) * BLK, BLK), F32),
-        in_specs=[SMEM] + [VMEM] * 6,
+        in_specs=[SMEM] + [ANY] * 4 + [VMEM] * 4,
         out_specs=VMEM,
-        compiler_params=params(),
-        cost_estimate=cost(0, 1 << 20),
-    )(meta, fs, fd, *xs)
+        scratch_shapes=[pltpu.SemaphoreType.DMA(())],
+        compiler_params=params(),
+        cost_estimate=cost(0, 1 << 20),
+    )(meta, *fs, *xs)
 
 
 def dot(a, b, dims=((1,), (0,))):
@@ -257,21 +330,29 @@
     sub = lax.broadcasted_iota(jnp.int32, (8, BLK), 0)
     lane = lax.broadcasted_iota(jnp.int32, (8, BLK), 1)
     right = [(lane == sub + 8 * g).astype(F32) for g in range(groups)]
-    for k in range(BLK):
-        g0, kk = divmod(k, 8)
-        row_l = left[g0][kk : kk + 1, :]
-        row_r = right[g0][kk : kk + 1, :]
-        inv = 1.0 / row_l[:, k : k + 1]
-        row_l = row_l * inv
-        row_r = row_r * inv
-        for g in range(g0, groups):
-            if g == g0 and kk == 7:
-                continue
-            col = left[g][:, k : k + 1]
-            if g == g0:
-                col = jnp.where(sub[:, :1] > kk, col, 0.0)
-            left[g] = left[g] - col * row_l
-            right[g] = right[g] - col * row_r
+    for at in range(groups):
+        cols = [
+            {g: jnp.broadcast_to(left[g][:, k : k + 1], (8, BLK)) for g in range(at, groups)}
+            for k in range(8 * at, 8 * at + 8)
+        ]
+        row_l = [left[at][j : j + 1, :] for j in range(8)]
+        row_r = [right[at][j : j + 1, :] for j in range(8)]
+        for j in range(8):
+            inv = 1.0 / cols[j][at][j : j + 1, :]
+            row_l[j] = row_l[j] * inv
+            row_r[j] = row_r[j] * inv
+            for m in range(j + 1, 8):
+                entry = cols[j][at][m : m + 1, :]
+                row_l[m] = row_l[m] - entry * row_l[j]
+                row_r[m] = row_r[m] - entry * row_r[j]
+                scaled = entry * inv
+                for g in range(at, groups):
+                    cols[m][g] = cols[m][g] - cols[j][g] * scaled
+        for g in range(at, groups):
+            for j in range(8):
+                col = cols[j][g] if g > at else jnp.where(sub > j, cols[j][g], 0.0)
+                left[g] = left[g] - col * row_l[j]
+                right[g] = right[g] - col * row_r[j]
     out = []
     for g in range(groups):
         diag = jnp.sum(jnp.where(lane == sub + 8 * g, left[g], 0.0), axis=1, keepdims=True)
@@ -308,56 +389,36 @@
     return 0.5 * (d + d.T)
 
 
-def first_kernel(meta, own, got, w0, l10, rest, tick, a, low, w):
+def factor_kernel(meta, own, got, w0, l10, w1, tick, a, low, w):
     s = meta[1]
     d = jnp.concatenate([pick(s, own, got, q) for q in range(4)], axis=1)
     a[...] = symmetric(d[:PW, :PW])
     inverse_panel(a, low, w, w0)
     below = dot_t(d[PW:, :PW], w0[...])
     l10[...] = below
-    rest[...] = symmetric(d[PW:, PW:] - dot_t(below, below))
-    tick[...] = jnp.zeros_like(tick)
-
-
-def second_kernel(rest, _, w1, tick, a, low, w):
-    a[...] = rest[...]
+    a[...] = symmetric(d[PW:, PW:] - dot_t(below, below))
     inverse_panel(a, low, w, w1)
     tick[...] = jnp.zeros_like(tick)
 
 
-FACTOR_SCRATCH = [
-    pltpu.VMEM((PW, PW), F32),
-    pltpu.VMEM((BLK, BLK), F32),
-    pltpu.VMEM((2, BLK, BLK), F32),
-]
-
-
-def factor_first(meta, own, got):
+def factor(meta, own, got):
     shape = jax.ShapeDtypeStruct((PW, PW), F32)
     diag = pl.BlockSpec((2, 2 * PW, BLK), lambda i: (0, 3, 0))
     whole = pl.BlockSpec((PW, PW), lambda i: (0, 0))
     return pl.pallas_call(
-        first_kernel,
+        factor_kernel,
         grid=(1,),
         out_shape=(shape, shape, shape, TICK),
         in_specs=[SMEM, diag, diag],
         out_specs=(whole, whole, whole, pl.BlockSpec((8, BLK), lambda i: (0, 0))),
-        scratch_shapes=FACTOR_SCRATCH,
+        scratch_shapes=[
+            pltpu.VMEM((PW, PW), F32),
+            pltpu.VMEM((BLK, BLK), F32),
+            pltpu.VMEM((2, BLK, BLK), F32),
+        ],
         compiler_params=params(),
         cost_estimate=cost(0, 90 << 20),
     )(meta, own, got)
-
-
-def factor_second(rest, tick):
-    return pl.pallas_call(
-        second_kernel,
-        out_shape=(jax.ShapeDtypeStruct((PW, PW), F32), TICK),
-        in_specs=[VMEM, VMEM],
-        out_specs=(VMEM, VMEM),
-        scratch_shapes=FACTOR_SCRATCH,
-        compiler_params=params(),
-        cost_estimate=cost(0, 90 << 20),
-    )(rest, tick)
 
 
 def split(x):
@@ -371,7 +432,8 @@
     return first, second
 
 
-def rows_kernel(meta, own, got, w0, l10, w1, _, low, high, rest):
+def rows_kernel(meta, own, got, w0, l10, w1, _, low, high, rest, tick):
+    tick[...] = jnp.zeros_like(tick)
     i = pl.program_id(0)
     x = jnp.concatenate([pick(meta[1], own, got, q) for q in range(4)], axis=1)
     first, second = solve(x, w0[...], l10[...], w1[...])
@@ -393,15 +455,16 @@
             jax.ShapeDtypeStruct((n, 2 * PW), F32),
             jax.ShapeDtypeStruct((n, 2 * PW), jnp.bfloat16),
             jax.ShapeDtypeStruct((n, 2 * PW), jnp.bfloat16),
+            TICK,
         ),
         in_specs=[SMEM, src, src, whole, whole, whole, pl.BlockSpec((8, BLK), lambda i: (0, 0))],
-        out_specs=(out, out, out),
+        out_specs=(out, out, out, pl.BlockSpec((8, BLK), lambda i: (0, 0))),
         compiler_params=params(),
         cost_estimate=cost(0, 1 << 20),
     )(meta, own, got, w0, l10, w1, tick)
 
 
-def cols_kernel(meta, o0, g0, o1, g1, o2, g2, o3, g3, w0, l10, w1, high, rest):
+def cols_kernel(meta, o0, g0, o1, g1, o2, g2, o3, g3, w0, l10, w1, _, high, rest):
     r, s = meta[0], meta[1]
     away = lax.rem(r - s + ROWS, ROWS)
     owns, gots = (o0, o1, o2, o3), (g0, g1, g2, g3)
@@ -422,7 +485,7 @@
     high[...], rest[...] = split(whole)
 
 
-def factor_cols(meta, pairs, w0, l10, w1):
+def factor_cols(meta, pairs, w0, l10, w1, tick):
     n = PB * BLK
 
     def src(d):
@@ -438,57 +501,57 @@
         grid_spec=pltpu.PrefetchScalarGridSpec(
             num_scalar_prefetch=1,
             grid=(n // PW,),
-            in_specs=[src(d) for d in range(ROWS) for _ in range(2)] + [whole] * 3,
+            in_specs=[src(d) for d in range(ROWS) for _ in range(2)]
+            + [whole] * 3
+            + [pl.BlockSpec((8, BLK), lambda i, meta: (0, 0))],
             out_specs=(out, out),
         ),
         out_shape=(jax.ShapeDtypeStruct((2 * PW, n), jnp.bfloat16),) * 2,
         compiler_params=params(),
         cost_estimate=cost(0, 1 << 20),
-    )(meta, *[x for pair in pairs for x in pair], w0, l10, w1)
+    )(meta, *[x for pair in pairs for x in pair], w0, l10, w1, tick)
 
 
 def table_kernel(meta, out):
-    for n in range(6 * PB + 16):
+    for n in range(6 * PB + 8):
         out[n] = jnp.int32(-1)
     for c in range(2):
         base = OWN + 24 * c
         for axis in range(2):
             here = meta[axis]
             for sender in range(ROWS):
+                if c == 0:
+                    source = jnp.int32(sender)
+                elif axis == 0:
+                    source = lax.rem(here - sender + ROWS, ROWS)
+                else:
+                    source = jnp.bitwise_xor(here, sender)
                 targets, ranks, places = ranked(meta, base, sender)
                 for i in range(CB):
 
                     @pl.when(targets[i] == here)
                     def _():
-                        out[(3 * c + axis) * PB + places[i]] = CAP * sender + ranks[i]
-                        if c == 1 and axis == 0:
-                            out[6 * PB + CAP * sender + ranks[i]] = places[i]
+                        out[(3 * c + axis) * PB + places[i]] = CAP * source + ranks[i]
+                        if c == 1 and axis == 1:
+                            out[6 * PB + CAP * source + ranks[i]] = places[i]
 
         last = jnp.int32(0)
         for p in range(PB):
             slot = out[3 * c * PB + p]
             last = jnp.where(slot >= 0, slot, last)
             out[(3 * c + 2) * PB + p] = last
-    first = jnp.int32(0)
-    for j in reversed(range(8)):
-        first = jnp.where(out[6 * PB + j] >= 0, out[6 * PB + j], first)
-    for j in range(8):
-        at = out[6 * PB + j]
-        out[6 * PB + 8 + j] = (at >= 0).astype(jnp.int32)
-        first = jnp.where(at >= 0, at, first)
-        out[6 * PB + j] = first
 
 
 def tables(meta):
     return pl.pallas_call(
         table_kernel,
-        out_shape=jax.ShapeDtypeStruct((6 * PB + 16,), jnp.int32),
+        out_shape=jax.ShapeDtypeStruct((6 * PB + 8,), jnp.int32),
         in_specs=[SMEM],
         out_specs=SMEM,
     )(meta)
 
 
-def trail_kernel(meta, tab, front, xa, low, rh, rl, ch, cl, out):
+def trail_kernel(meta, tab, front, xa, y0, y1, y2, y3, low, rh, rl, ch, cl, out):
     p = pl.program_id(0)
     r, s = meta[0], meta[1]
     top = (r == 0) & (p < 4)
@@ -506,26 +569,42 @@
             at = slice(c * PW, (c + 1) * PW)
             prod = mul(rh[...], ch[:, at]) + (mul(rh[...], cl[:, at]) + mul(rl[...], ch[:, at]))
             out[:, at] = front[:, at] - prod
-        there = tab[p] >= 0
-        for q in range(PB):
-            slot = tab[PB + q]
-
-            @pl.when(there & (slot >= 0))
-            def _():
-                at = slice(q * BLK, (q + 1) * BLK)
-                out[:, at] += xa[0, lax.div(slot, 2), 0, lax.rem(slot, 2)]
+
+        @pl.when(tab[p] >= 0)
+        def _():
+            for q in range(PB):
+                slot = tab[PB + q]
+
+                @pl.when(slot >= 0)
+                def _():
+                    at = slice(q * BLK, (q + 1) * BLK)
+                    out[:, at] += xa[0, lax.div(slot, 2), 0, lax.rem(slot, 2)]
+
+        @pl.when(tab[3 * PB + p] >= 0)
+        def _():
+            for m, y in enumerate((y0, y1, y2, y3)):
+                for k in range(CAP):
+                    q = tab[6 * PB + m * CAP + k]
+
+                    @pl.when(q >= 0)
+                    def _():
+                        at = pl.ds(pl.multiple_of(q * BLK, BLK), BLK)
+                        out[:, at] += y[0, k]
 
     @pl.when(s == 0)
     def _():
         out[:, : 2 * PW] = low[...]
 
 
-def trail(meta, tab, front, xa, low, rh, rl, ch, cl):
+def trail(meta, tab, front, xa, ys, low, rh, rl, ch, cl):
     n = PB * BLK
 
-    def index(p, meta, tab):
+    def of_a(p, meta, tab):
         slot = tab[2 * PB + p]
         return (lax.div(slot, 2), 0, lax.rem(slot, 2), 0, 0, 0)
+
+    def of_b(p, meta, tab):
+        return (tab[5 * PB + p], 0, 0, 0)
 
     wide = pl.BlockSpec((BLK, n), lambda p, meta, tab: (p, 0))
     rows = pl.BlockSpec((BLK, 2 * PW), lambda p, meta, tab: (p, 0))
@@ -535,57 +614,15 @@
         grid_spec=pltpu.PrefetchScalarGridSpec(
             num_scalar_prefetch=2,
             grid=(PB,),
-            in_specs=[wide, pl.BlockSpec((1, 4, 1, 2, BLK, BLK), index)]
+            in_specs=[wide, pl.BlockSpec((1, 4, 1, 2, BLK, BLK), of_a)]
+            + [pl.BlockSpec((1, CAP, BLK, BLK), of_b)] * 4
             + [rows, rows, rows, cols, cols],
             out_specs=wide,
         ),
         out_shape=jax.ShapeDtypeStruct((n, n), F32),
         compiler_params=params(),
         cost_estimate=cost(0, 1 << 20),
-    )(meta, tab, front, xa, low, rh, rl, ch, cl)
-
-
-def last_kernel(meta, tab, front, xb, out):
-    j = pl.program_id(0)
-    p = tab[6 * PB + j]
-    fresh = (j == 0) | (p != tab[6 * PB + jnp.maximum(j - 1, 0)])
-
-    @pl.when(fresh)
-    def _():
-        out[...] = front[...]
-
-    add = (tab[6 * PB + 8 + j] > 0) & jnp.logical_not((meta[0] == 0) & (p < 4))
-    for q in range(PB):
-        slot = tab[4 * PB + q]
-
-        @pl.when(add & (slot >= 0) & ((meta[1] > 0) | (q >= 4)))
-        def _():
-            at = slice(q * BLK, (q + 1) * BLK)
-            out[:, at] += xb[0, lax.div(slot, 2), 0, lax.rem(slot, 2)]
-
-
-def last(meta, tab, front, xb):
-    n = PB * BLK
-    wide = pl.BlockSpec((BLK, n), lambda j, meta, tab: (tab[6 * PB + j], 0))
-    return pl.pallas_call(
-        last_kernel,
-        grid_spec=pltpu.PrefetchScalarGridSpec(
-            num_scalar_prefetch=2,
-            grid=(2 * ROWS,),
-            in_specs=[
-                wide,
-                pl.BlockSpec(
-                    (1, 4, 1, 2, BLK, BLK),
-                    lambda j, meta, tab: (lax.div(j, 2), 0, lax.rem(j, 2), 0, 0, 0),
-                ),
-            ],
-            out_specs=wide,
-        ),
-        out_shape=jax.ShapeDtypeStruct((n, n), F32),
-        input_output_aliases={2: 0},
-        compiler_params=params(),
-        cost_estimate=cost(0, 1 << 20),
-    )(meta, tab, front, xb)
+    )(meta, tab, front, xa, *ys, low, rh, rl, ch, cl)
 
 
 def move(x, axes, fn, sizes, only=None):
@@ -639,29 +676,43 @@
 
     sibling = across_cube(child)
 
-    fs = [front[:, q * BLK : (q + 1) * BLK] for q in range(4)]
-    moved = [move(fs[q], ("col",), lambda s: (q,), (4,), lambda s: s == 0) for q in range(1, 4)]
+    corner = front[: 2 * PW, : 2 * PW]
+    corners = [
+        move(corner, ("row", "col"), lambda r, s: (d, 0), (4, 4), lambda r, s: r == 0 and s == 0)
+        for d in range(1, 4)
+    ]
     xa = exchange(pack(meta, child, OWN, meta))
 
     keep, send = strips(meta, child, sibling)
     got = across_col(send, 1)
+    got, *rows = barrier((got, *row_pack(meta, sibling, OWN + 24)))
     chosen = choose(meta, keep, got)
     far = across_col(chosen, 2)
-    xa, far = barrier((xa, far))
+    corner, corners, _ = barrier((corner, corners, chosen))
+    corner = jnp.where(row_here == 0, corner, corners[0] + corners[1] + corners[2])
+    wide = jnp.concatenate([front[:, : 2 * PW], corner], axis=0)
+    fs = [wide[:, q * BLK : (q + 1) * BLK] for q in range(4)]
+    fs = [fs[0]] + [
+        move(fs[q], ("col",), lambda s: (q,), (4,), lambda s: s == 0) for q in range(1, 4)
+    ]
+    rows = [rows[0]] + [
+        move(rows[d], ("row",), lambda r: ((r + d) % 4,), (4,)) for d in range(1, 4)
+    ]
+    tab = tables(meta)
+    xa, far, tab, *rows = barrier((xa, far, tab, *rows))
     outs = band(meta, keep, got, far)
-    moved, outs = barrier((moved, outs))
-    fs = jnp.where(col_here == 0, fs[0], moved[0] + moved[1] + moved[2])
-    top = fs[: 2 * PW]
-    tops = [move(top, ("row",), lambda r: (d,), (4,), lambda r: r == 0) for d in range(1, 4)]
-    fd = jnp.where(row_here == 0, top, tops[0] + tops[1] + tops[2])
     xs = [outs[0]] + [
         move(outs[d], ("row",), lambda r: ((r + d) % 4,), (4,)) for d in range(1, 4)
     ]
-    mine = strip_add(meta, fs, fd, xs)
-
-    own = jnp.stack([mine, across_col(mine, 2)])
+    mine = strip_add(meta, fs, xs)
+
+    far = across_col(mine, 2)
+    mine, *rows = barrier((mine, *rows))
+    cols = col_pack(meta, rows, OWN + 24)
+    mine, far, *cols = barrier((mine, far, *cols))
+    own = jnp.stack([mine, far])
     other = across_col(own, 1)
-    tab = tables(meta)
+    ys = [cols[0]] + [across_col(cols[m], m) for m in range(1, 4)]
 
     def step(x, start, stop):
         return move(
@@ -675,22 +726,17 @@
     own_band, other_band = own[:, :n], other[:, :n]
     o1, o3 = step(own_band, 0, 1), step(own_band, 0, 3)
     g1, g3 = step(other_band, 0, 1), step(other_band, 0, 3)
-    w0, l10, rest, tick = factor_first(meta, own, other)
+    w0, l10, w1, tick = factor(meta, own, other)
     tick = across_col(tick, 1)
-    o1, o3, g1, g3, rest, tick = barrier((o1, o3, g1, g3, rest, tick))
+    o1, o3, g1, g3, w1, tick, ys[1], ys[2] = barrier((o1, o3, g1, g3, w1, tick, ys[1], ys[2]))
     o2, g2 = step(o1, 1, 2), step(g3, 3, 2)
-    w1, tick = factor_second(rest, tick)
+    low, rh, rl, tick = factor_rows(meta, own, other, w0, l10, w1, tick)
     tick = across_col(tick, 1)
-    w0, l10, w1, tick, o2, g2, sibling = barrier((w0, l10, w1, tick, o2, g2, sibling))
-    packed = pack(meta, sibling, OWN + 24, tick)
-    packed, w1 = barrier((packed, w1))
-    xb = exchange(packed)
-    low, rh, rl = factor_rows(meta, own, other, w0, l10, w1, tick)
+    tick, o2, g2, ys[3] = barrier((tick, o2, g2, ys[3]))
     ch, cl = factor_cols(
-        meta, ((own, other), (o1, g1), (o2, g2), (o3, g3)), w0, l10, w1
+        meta, ((own, other), (o1, g1), (o2, g2), (o3, g3)), w0, l10, w1, tick
     )
-    whole = trail(meta, tab, front, xa, low, rh, rl, ch, cl)
-    return last(meta, tab, whole, xb)[None]
+    return trail(meta, tab, front, xa, ys, low, rh, rl, ch, cl)[None]
 
 
 def solution(mesh):

time: 313 us -> 293 us (0.936)
  Pallas kernels: 129 us -> 91.9 us
  waiting for transfers between devices: 108 us -> 132 us
  starting transfers between devices: 62.1 us -> 47.4 us
  local copies, waits for them, and re-layouts: 7.74 us -> 11 us
    ppermute x22 -> x28, waiting for transfers between devices: 94.9 us -> 132 us  [move(): return lax.ppermute(x, axes if len(axes) > 1 else axes[0], pairs)]
    pallas_call x4, Pallas kernels: 61.7 us -> 28.4 us  [the longest x1 19.4 us: factor(): pl.pallas_call(factor_kernel, grid=(1,), out_shape=(shape, shape, shape,...]
    all_to_all x2 -> x1, waiting for transfers between devices: 13 us -> 0.01 us  [exchange(): lax.all_to_all(packed.reshape(16, per, BLK, BLK), ('row', 'col'), 0, 0, t...]
    all_to_all x2 -> x1, starting transfers between devices: 16.8 us -> 7.83 us  [exchange(): lax.all_to_all(packed.reshape(16, per, BLK, BLK), ('row', 'col'), 0, 0, t...]
    ppermute x22 -> x28, starting transfers between devices: 45.3 us -> 39.6 us  [move(): return lax.ppermute(x, axes if len(axes) > 1 else axes[0], pairs)]
    pallas_call x2 -> x1, Pallas kernels: 7.39 us -> 3.38 us  [pack(): pl.pallas_call(functools.partial(pack_kernel, base), out_shape=jax.ShapeD...]
  transfers between devices with their start and end apart: 24 -> 29, of which waited for: 10 -> 13; matrix products, arithmetic and copies ran while one was open for 1% -> 4% of each run, Pallas kernels for 36% -> 19%
where the time goes in v2:
time: 293 us; the launch traced here: 290 us
  waiting for transfers between devices  132 us (45%)
  Pallas kernels  91.9 us (31%)
  starting transfers between devices  47.4 us (16%)
  local copies, waits for them, and re-layouts  11 us (4%)
  other arithmetic  6.49 us (2%)
    ppermute x28, waiting for transfers between devices, move(): return lax.ppermute(x, axes if len(axes) > 1 else axes[0], pairs)  132 us
    ppermute x28, starting transfers between devices, move(): return lax.ppermute(x, axes if len(axes) > 1 else axes[0], pairs)  39.6 us
    pallas_call x1, Pallas kernels, trail(): pl.pallas_call(trail_kernel, grid_spec=pltpu.PrefetchScalarGridSpec(num_s...  20.4 us
    pallas_call x1, Pallas kernels, factor(): pl.pallas_call(factor_kernel, grid=(1,), out_shape=(shape, shape, shape,...  19.4 us
    pallas_call x1, Pallas kernels, factor_cols(): pl.pallas_call(cols_kernel, grid_spec=pltpu.PrefetchScalarGridSpec(num_sc...  13.4 us
    pallas_call x1, Pallas kernels, factor_rows(): pl.pallas_call(rows_kernel, grid=(n // PW,), out_shape=(jax.ShapeDtypeStr...  10.7 us
    all_to_all x1, starting transfers between devices, exchange(): lax.all_to_all(packed.reshape(16, per, BLK, BLK), ('row', 'col'), 0, 0, t...  7.83 us
  transfers between devices with their start and end apart: 29, of which 13 were waited for; matrix products, arithmetic and copies ran while one was open for 4% of the time, Pallas kernels for 19%

profile of v2, /device:TPU:85, one launch (start us, length us, event | category | flops | bytes accessed | tf_op | source)
XLA Modules:
  0.0 289.6 jit_solution(4009994686801201940)
XLA Ops:
  2.7 3.4 %shard_map.37 = f32[64,128,128]{2,1,0:T(8,128)} custom-call(s32[50]{0:T(128)} %pad_add_fusion.meta._, f32[768,768]{1,0:T(8,128)} %bitcast.14, s32[50]{0:T(128)} %pad_add_fusion.meta._), custom_call_target="tpu_custom_call" | custom-call | bytes 1048576 | tf_op jit(solution)/shard_map/pallas_call | solution.py:72
  6.1 7.8 %all-to-all-start = ((f32[16,4,128,128]{3,2,1,0:T(8,128)}), f32[16,4,128,128]{3,2,1,0:T(8,128)}, u32[]{:S(2)}, u32[]{:S(2)}) async-start(f32[16,4,128,128]{3,2,1,0:T(8,128)} %bitcast.12), calls=%async_computation | async-start | bytes 8388608 | tf_op jit(solution)/shard_map/all_to_all | solution.py:664
  13.9 38.5 %collective-permute-done.sibling.child = f32[768,768]{1,0:T(8,128)S(1)} collective-permute-done((f32[768,768]{1,0:T(8,128)}, f32[768,768]{1,0:T(8,128)S(1)}, u32[]{:S(2)}, u32[]{:S(2)}) %collective-permute-start) | collective-permute-done | bytes 2359328 | tf_op jit(solution)/shard_map/ppermute | solution.py:651
  53.9 4.2 %shard_map.38 = (f32[2,2,768,128]{3,2,1,0:T(8,128)}, f32[2,2,768,128]{3,2,1,0:T(8,128)}) custom-call(s32[50]{0:T(128)} %pad_add_fusion.meta._, f32[768,768]{1,0:T(8,128)} %bitcast.15, f32[768,768]{1,0:T(8,128)} %copy-done.2), custom_call_target="tpu_custom_call" | custom-call | bytes 1048576 | tf_op jit(solution)/shard_map/pallas_call | solution.py:174
  59.5 2.3 slice.33
  66.8 2.2 slice.32
  69.0 3.2 %shard_map.39 = (f32[2,128,768]{2,1,0:T(8,128)}, f32[2,128,768]{2,1,0:T(8,128)}, f32[2,128,768]{2,1,0:T(8,128)}, f32[2,128,768]{2,1,0:T(8,128)}) custom-call(s32[50]{0:T(128)} %pad_add_fusion.meta._, f32[768,768]{1,0:T(8,128)} %copy-done.2), custom_call_target="tpu_custom_call" | custom-call | bytes 1048576 | tf_op jit(solution)/shard_map/pallas_call | solution.py:103
  72.2 2.9 shard_map.40
  76.1 2.4 add_select_fusion
  78.5 2.2 pad_maximum_fusion.1
  82.8 13.1 %collective-permute-done.2.far = f32[2,768,128]{2,1,0:T(8,128)S(1)} collective-permute-done((f32[2,768,128]{2,1,0:T(8,128)}, f32[2,768,128]{2,1,0:T(8,128)S(1)}, u32[]{:S(2)}, u32[]{:S(2)}) %collective-permute-start.2) | collective-permute-done | bytes 786464 | tf_op jit(solution)/shard_map/ppermute | solution.py:651
  100.4 1.8 shard_map.41.tab
  102.2 7.8 %collective-permute-done.4.x2 = f32[2,128,768]{2,1,0:T(8,128)} collective-permute-done((f32[2,128,768]{2,1,0:T(8,128)}, f32[2,128,768]{2,1,0:T(8,128)}, u32[]{:S(2)}, u32[]{:S(2)}) %collective-permute-start.4) | collective-permute-done | bytes 786464 | tf_op jit(solution)/shard_map/ppermute | solution.py:651
  110.0 6.5 %collective-permute-done.5.x3 = f32[2,128,768]{2,1,0:T(8,128)} collective-permute-done((f32[2,128,768]{2,1,0:T(8,128)}, f32[2,128,768]{2,1,0:T(8,128)}, u32[]{:S(2)}, u32[]{:S(2)}) %collective-permute-start.5) | collective-permute-done | bytes 786464 | tf_op jit(solution)/shard_map/ppermute | solution.py:651
  116.5 4.8 %shard_map.42 = (f32[8,128,128]{2,1,0:T(8,128)}, f32[8,128,128]{2,1,0:T(8,128)}, f32[8,128,128]{2,1,0:T(8,128)}, f32[8,128,128]{2,1,0:T(8,128)}) custom-call(s32[50]{0:T(128)} %pad_add_fusion.meta._, f32[2,2,768,128]{3,2,1,0:T(8,128)} %get-tuple-element.68.keep, f32[2,2,768,128]{3,2,1,0:T(8,128)} %collective-permute-done.1.got, f32[2,768,128]{2,1,0:T(8,128)} %copy-done.13), custom_call_target="tpu_custom_call" | custom-call | bytes 1048576 | tf_op jit(solution)/shard_map/pallas_call | solution.py:268
  121.4 3.7 %collective-permute-start.12 = (f32[8,128,128]{2,1,0:T(8,128)}, f32[8,128,128]{2,1,0:T(8,128)S(1)}, u32[]{:S(2)}, u32[]{:S(2)}) collective-permute-start(f32[8,128,128]{2,1,0:T(8,128)} %get-tuple-element.87), channel_id=1, source_target_pairs={{0,4},{4,8},{8,12},{12,0},{1,5},{5,9},{9,13},{13,1},{2,6},{6,10},{... | collective-permute-start | bytes 1572872 | tf_op jit(solution)/shard_map/ppermute | solution.py:651
  126.4 3.7 %collective-permute-done.11.f3 = f32[2048,128]{1,0:T(8,128)S(1)} collective-permute-done((f32[2048,128]{1,0:T(8,128)}, f32[2048,128]{1,0:T(8,128)S(1)}, u32[]{:S(2)}, u32[]{:S(2)}) %collective-permute-start.11) | collective-permute-done | bytes 1048608 | tf_op jit(solution)/shard_map/ppermute | solution.py:651
  130.1 6.1 %collective-permute-done.12.x1 = f32[8,128,128]{2,1,0:T(8,128)S(1)} collective-permute-done((f32[8,128,128]{2,1,0:T(8,128)}, f32[8,128,128]{2,1,0:T(8,128)S(1)}, u32[]{:S(2)}, u32[]{:S(2)}) %collective-permute-start.12) | collective-permute-done | bytes 524320 | tf_op jit(solution)/shard_map/ppermute | solution.py:651
  136.3 11.2 %collective-permute-done.13.x2 = f32[8,128,128]{2,1,0:T(8,128)S(1)} collective-permute-done((f32[8,128,128]{2,1,0:T(8,128)}, f32[8,128,128]{2,1,0:T(8,128)S(1)}, u32[]{:S(2)}, u32[]{:S(2)}) %collective-permute-start.13) | collective-permute-done | bytes 524320 | tf_op jit(solution)/shard_map/ppermute | solution.py:651
  149.6 3.7 %shard_map.43 = f32[2048,128]{1,0:T(8,128)} custom-call(s32[50]{0:T(128)} %pad_add_fusion.meta._, f32[2048,128]{1,0:T(8,128)} %get-tuple-element.132.f0, f32[2048,128]{1,0:T(8,128)} %copy-done.8, f32[2048,128]{1,0:T(8,128)} %copy-done.9, f32[2048,128]{1,0:T(8,128)} %copy-done.10, f32[8,128,128]{2,1,0:T(8,128)} %get-tuple-element.86.x0, ...), custom_call_target="tpu_custom_call" | custom-call | bytes 1048576 | tf_op jit(solution)/shard_map/pallas_call | solution.py:308
  154.3 4.0 %shard_map.44 = (f32[8,2,128,128]{3,2,1,0:T(8,128)}, f32[8,2,128,128]{3,2,1,0:T(8,128)}, f32[8,2,128,128]{3,2,1,0:T(8,128)}, f32[8,2,128,128]{3,2,1,0:T(8,128)}) custom-call(s32[50]{0:T(128)} %pad_add_fusion.meta._, f32[2,128,768]{2,1,0:T(8,128)} %get-tuple-element.95.x0, f32[2,128,768]{2,1,0:T(8,128)} %copy-done.14, ...), custom_call_target="tpu_custom_call" | custom-call | bytes 1048576 | tf_op jit(solution)/shard_map/pallas_call | solution.py:139
  158.3 19.1 %collective-permute-done.15 = f32[2048,128]{1,0:T(8,128)S(1)} collective-permute-done((f32[2048,128]{1,0:T(8,128)}, f32[2048,128]{1,0:T(8,128)S(1)}, u32[]{:S(2)}, u32[]{:S(2)}) %collective-permute-start.15) | collective-permute-done | bytes 1048608 | tf_op jit(solution)/shard_map/ppermute | solution.py:651
  177.6 3.4 %collective-permute-start.18 = (f32[2,2048,128]{2,1,0:T(8,128)S(1)}, f32[2,2048,128]{2,1,0:T(8,128)S(1)}, u32[]{:S(2)}, u32[]{:S(2)}) collective-permute-start(f32[2,2048,128]{2,1,0:T(8,128)S(1)} %pad_maximum_fusion.own.o0), channel_id=1, source_target_pairs={{0,1},{1,0},{2,3},{3,2},{4,5},{5,4},{6,7},{7,6},{8,9},{9,8},{10,11... | collective-permute-start | bytes 6291464 | tf_op jit(solution)/shard_map/ppermute | solution.py:651
  189.2 1.9 collective-permute-start.23
  191.1 19.4 %shard_map.45 = (f32[256,256]{1,0:T(8,128)}, f32[256,256]{1,0:T(8,128)}, f32[256,256]{1,0:T(8,128)}, f32[8,128]{1,0:T(8,128)}) custom-call(s32[50]{0:T(128)} %pad_add_fusion.meta._, f32[2,2048,128]{2,1,0:T(8,128)} %copy-done, f32[2,2048,128]{2,1,0:T(8,128)} %copy-done.1), custom_call_target="tpu_custom_call" | custom-call | bytes 94371840 | tf_op jit(solution)/shard_map/pallas_call | solution.py:408
  210.5 6.3 %collective-permute-start.21 = (f32[8,128]{1,0:T(8,128)}, f32[8,128]{1,0:T(8,128)S(1)}, u32[]{:S(2)}, u32[]{:S(2)}) collective-permute-start(f32[8,128]{1,0:T(8,128)} %get-tuple-element.107), channel_id=1, source_target_pairs={{0,1},{1,0},{2,3},{3,2},{4,5},{5,4},{6,7},{7,6},{8,9},{9,8},{10,11... | collective-permute-start | bytes 12296 | tf_op jit(solution)/shard_map/ppermute | solution.py:651
  217.9 7.4 %collective-permute-done.20.g3 = f32[2,1536,128]{2,1,0:T(8,128)} collective-permute-done((f32[2,1536,128]{2,1,0:T(8,128)}, f32[2,1536,128]{2,1,0:T(8,128)}, u32[]{:S(2)}, u32[]{:S(2)}) %collective-permute-start.20) | collective-permute-done | bytes 1572896 | tf_op jit(solution)/shard_map/ppermute | solution.py:651
  226.0 2.4 collective-permute-start.26
  228.5 10.7 %shard_map.46 = (f32[1536,512]{1,0:T(8,128)}, bf16[1536,512]{1,0:T(8,128)(2,1)}, bf16[1536,512]{1,0:T(8,128)(2,1)}, f32[8,128]{1,0:T(8,128)}) custom-call(s32[50]{0:T(128)} %pad_add_fusion.meta._, f32[2,2048,128]{2,1,0:T(8,128)} %copy-done, f32[2,2048,128]{2,1,0:T(8,128)} %copy-done.1, f32[256,256]{1,0:T(8,128)} %get-tuple-element.112.w0, ...), custom_call_target="tpu_custom_call" | custom-call | bytes 1048576 | tf_op jit(solution)/shard_map/pallas_call | solution.py:451
  239.5 15.0 %collective-permute-done.27.y3 = f32[8,2,128,128]{3,2,1,0:T(8,128)S(1)} collective-permute-done((f32[8,2,128,128]{3,2,1,0:T(8,128)}, f32[8,2,128,128]{3,2,1,0:T(8,128)S(1)}, u32[]{:S(2)}, u32[]{:S(2)}) %collective-permute-start.27) | collective-permute-done | bytes 1048608 | tf_op jit(solution)/shard_map/ppermute | solution.py:651
  255.8 13.4 %shard_map.47 = (bf16[512,1536]{1,0:T(8,128)(2,1)}, bf16[512,1536]{1,0:T(8,128)(2,1)}) custom-call(s32[50]{0:T(128)} %pad_add_fusion.meta._, f32[2,2048,128]{2,1,0:T(8,128)} %copy-done, f32[2,2048,128]{2,1,0:T(8,128)} %copy-done.1, f32[2,1536,128]{2,1,0:T(8,128)} %copy-done.4, f32[2,1536,128]{2,1,0:T(8,128)} %copy-done.6, f32[2,1536,128]{2,1,0:T(8,128)} %copy-done.7, ...), custom_call_target="tpu_custom_call" | custom-call | bytes 1048576 | tf_op jit(solution)/shard_map/pallas_call | solution.py:499
  269.2 20.4 %shard_map.48 = f32[1536,1536]{1,0:T(8,128)} custom-call(s32[50]{0:T(128)} %pad_add_fusion.meta._, s32[80]{0:T(128)} %shard_map.41.tab, f32[1536,1536]{1,0:T(8,128)} %bitcast.11, f32[4,4,2,2,128,128]{5,4,3,2,1,0:T(8,128)} %bitcast.4.xa, f32[8,2,128,128]{3,2,1,0:T(8,128)} %get-tuple-element.103.y0, f32[8,2,128,128]{3,2,1,0:T(8,128)} %copy-done.11, ...), custom_call_target="tpu_custom_call" | custom-call | bytes 1048576 | tf_op jit(solution)/shard_map/pallas_call | solution.py:612
  (91 shorter events, 34.2 us)
Async XLA Ops:
  0.0 52.4 %collective-permute-start = (f32[768,768]{1,0:T(8,128)}, f32[768,768]{1,0:T(8,128)S(1)}, u32[]{:S(2)}, u32[]{:S(2)}) collective-permute-start(f32[768,768]{1,0:T(8,128)} %bitcast.13), channel_id=1, source_target_pairs={{0,16},{16,0},{32,48},{48,32},{64,80},{80,64},{96,112},{112,96},{1... | collective-permute-start | bytes 7077896 | tf_op jit(solution)/shard_map/ppermute | solution.py:651
  6.1 96.1 %all-to-all-start = ((f32[16,4,128,128]{3,2,1,0:T(8,128)}), f32[16,4,128,128]{3,2,1,0:T(8,128)}, u32[]{:S(2)}, u32[]{:S(2)}) async-start(f32[16,4,128,128]{3,2,1,0:T(8,128)} %bitcast.12), calls=%async_computation | async-start | bytes 8388608 | tf_op jit(solution)/shard_map/all_to_all | solution.py:664
  58.0 14.1 %collective-permute-start.1 = (f32[2,2,768,128]{3,2,1,0:T(8,128)}, f32[2,2,768,128]{3,2,1,0:T(8,128)}, u32[]{:S(2)}, u32[]{:S(2)}) collective-permute-start(f32[2,2,768,128]{3,2,1,0:T(8,128)} %get-tuple-element.69), channel_id=1, source_target_pairs={{0,1},{1,0},{2,3},{3,2},{4,5},{5,4},{6,7},{7,6},{8,9},{9,8},{10,11... | collective-permute-start | bytes 4718600 | tf_op jit(solution)/shard_map/ppermute | solution.py:651
  61.8 14.3 %collective-permute-start.6 = (f32[512,512]{1,0:T(8,128)}, f32[512,512]{1,0:T(8,128)}, u32[]{:S(2)}, u32[]{:S(2)}) collective-permute-start(f32[512,512]{1,0:T(8,128)} %slice.33), channel_id=1, source_target_pairs={{0,4},{16,20},{32,36},{48,52},{64,68},{80,84},{96,100},{112,116}} | collective-permute-start | bytes 3145736 | tf_op jit(solution)/shard_map/ppermute | solution.py:651
  63.5 12.6 %collective-permute-start.7 = (f32[512,512]{1,0:T(8,128)}, f32[512,512]{1,0:T(8,128)}, u32[]{:S(2)}, u32[]{:S(2)}) collective-permute-start(f32[512,512]{1,0:T(8,128)} %slice.33), channel_id=1, source_target_pairs={{0,8},{16,24},{32,40},{48,56},{64,72},{80,88},{96,104},{112,120}} | collective-permute-start | bytes 3145736 | tf_op jit(solution)/shard_map/ppermute | solution.py:651
  65.1 11.0 %collective-permute-start.8 = (f32[512,512]{1,0:T(8,128)}, f32[512,512]{1,0:T(8,128)}, u32[]{:S(2)}, u32[]{:S(2)}) collective-permute-start(f32[512,512]{1,0:T(8,128)} %slice.33), channel_id=1, source_target_pairs={{0,12},{16,28},{32,44},{48,60},{64,76},{80,92},{96,108},{112,124}} | collective-permute-start | bytes 3145736 | tf_op jit(solution)/shard_map/ppermute | solution.py:651
  75.0 21.0 %collective-permute-start.2 = (f32[2,768,128]{2,1,0:T(8,128)}, f32[2,768,128]{2,1,0:T(8,128)S(1)}, u32[]{:S(2)}, u32[]{:S(2)}) collective-permute-start(f32[2,768,128]{2,1,0:T(8,128)} %shard_map.40), channel_id=1, source_target_pairs={{0,2},{1,3},{2,0},{3,1},{4,6},{5,7},{6,4},{7,5},{8,10},{9,11},{10,... | collective-permute-start | bytes 2359304 | tf_op jit(solution)/shard_map/ppermute | solution.py:651
  75.2 23.0 %collective-permute-start.3 = (f32[2,128,768]{2,1,0:T(8,128)S(1)}, f32[2,128,768]{2,1,0:T(8,128)S(1)}, u32[]{:S(2)}, u32[]{:S(2)}) collective-permute-start(f32[2,128,768]{2,1,0:T(8,128)S(1)} %copy-done.21), channel_id=1, source_target_pairs={{0,4},{4,8},{8,12},{12,0},{1,5},{5,9},{9,13},{13,1},{2,6},{6,10},{... | collective-permute-start | bytes 2359304 | tf_op jit(solution)/shard_map/ppermute | solution.py:651
  80.6 44.6 %collective-permute-start.9 = (f32[2048,128]{1,0:T(8,128)}, f32[2048,128]{1,0:T(8,128)S(1)}, u32[]{:S(2)}, u32[]{:S(2)}) collective-permute-start(f32[2048,128]{1,0:T(8,128)} %get-tuple-element.133), channel_id=1, source_target_pairs={{0,1},{4,5},{8,9},{12,13},{16,17},{20,21},{24,25},{28,29},{32,33},... | collective-permute-start | bytes 3145736 | tf_op jit(solution)/shard_map/ppermute | solution.py:651
  81.4 28.7 %collective-permute-start.4 = (f32[2,128,768]{2,1,0:T(8,128)}, f32[2,128,768]{2,1,0:T(8,128)}, u32[]{:S(2)}, u32[]{:S(2)}) collective-permute-start(f32[2,128,768]{2,1,0:T(8,128)} %get-tuple-element.77), channel_id=1, source_target_pairs={{0,8},{4,12},{8,0},{12,4},{1,9},{5,13},{9,1},{13,5},{2,10},{6,14},... | collective-permute-start | bytes 2359304 | tf_op jit(solution)/shard_map/ppermute | solution.py:651
  82.3 34.3 %collective-permute-start.5 = (f32[2,128,768]{2,1,0:T(8,128)}, f32[2,128,768]{2,1,0:T(8,128)}, u32[]{:S(2)}, u32[]{:S(2)}) collective-permute-start(f32[2,128,768]{2,1,0:T(8,128)} %get-tuple-element.78), channel_id=1, source_target_pairs={{0,12},{4,0},{8,4},{12,8},{1,13},{5,1},{9,5},{13,9},{2,14},{6,2},{... | collective-permute-start | bytes 2359304 | tf_op jit(solution)/shard_map/ppermute | solution.py:651
  96.0 30.4 %collective-permute-start.10 = (f32[2048,128]{1,0:T(8,128)}, f32[2048,128]{1,0:T(8,128)S(1)}, u32[]{:S(2)}, u32[]{:S(2)}) collective-permute-start(f32[2048,128]{1,0:T(8,128)} %get-tuple-element.134), channel_id=1, source_target_pairs={{0,2},{4,6},{8,10},{12,14},{16,18},{20,22},{24,26},{28,30},{32,34}... | collective-permute-start | bytes 3145736 | tf_op jit(solution)/shard_map/ppermute | solution.py:651
  99.1 31.0 %collective-permute-start.11 = (f32[2048,128]{1,0:T(8,128)}, f32[2048,128]{1,0:T(8,128)S(1)}, u32[]{:S(2)}, u32[]{:S(2)}) collective-permute-start(f32[2048,128]{1,0:T(8,128)} %get-tuple-element.131), channel_id=1, source_target_pairs={{0,3},{4,7},{8,11},{12,15},{16,19},{20,23},{24,27},{28,31},{32,35}... | collective-permute-start | bytes 3145736 | tf_op jit(solution)/shard_map/ppermute | solution.py:651
  121.4 14.9 %collective-permute-start.12 = (f32[8,128,128]{2,1,0:T(8,128)}, f32[8,128,128]{2,1,0:T(8,128)S(1)}, u32[]{:S(2)}, u32[]{:S(2)}) collective-permute-start(f32[8,128,128]{2,1,0:T(8,128)} %get-tuple-element.87), channel_id=1, source_target_pairs={{0,4},{4,8},{8,12},{12,0},{1,5},{5,9},{9,13},{13,1},{2,6},{6,10},{... | collective-permute-start | bytes 1572872 | tf_op jit(solution)/shard_map/ppermute | solution.py:651
  125.1 22.4 %collective-permute-start.13 = (f32[8,128,128]{2,1,0:T(8,128)}, f32[8,128,128]{2,1,0:T(8,128)S(1)}, u32[]{:S(2)}, u32[]{:S(2)}) collective-permute-start(f32[8,128,128]{2,1,0:T(8,128)} %get-tuple-element.88), channel_id=1, source_target_pairs={{0,8},{4,12},{8,0},{12,4},{1,9},{5,13},{9,1},{13,5},{2,10},{6,14},... | collective-permute-start | bytes 1572872 | tf_op jit(solution)/shard_map/ppermute | solution.py:651
  125.2 23.6 %copy-start.8 = (f32[2048,128]{1,0:T(8,128)}, f32[2048,128]{1,0:T(8,128)S(1)}, u32[]{:S(2)}) copy-start(f32[2048,128]{1,0:T(8,128)S(1)} %collective-permute-done.9.f1) | copy-start | bytes 3145732
  125.2 23.6 %collective-permute-start.14 = (f32[8,128,128]{2,1,0:T(8,128)}, f32[8,128,128]{2,1,0:T(8,128)S(1)}, u32[]{:S(2)}, u32[]{:S(2)}) collective-permute-start(f32[8,128,128]{2,1,0:T(8,128)} %get-tuple-element.89), channel_id=1, source_target_pairs={{0,12},{4,0},{8,4},{12,8},{1,13},{5,1},{9,5},{13,9},{2,14},{6,2},{... | collective-permute-start | bytes 1572872 | tf_op jit(solution)/shard_map/ppermute | solution.py:651
  126.4 22.4 %copy-start.9 = (f32[2048,128]{1,0:T(8,128)}, f32[2048,128]{1,0:T(8,128)S(1)}, u32[]{:S(2)}) copy-start(f32[2048,128]{1,0:T(8,128)S(1)} %collective-permute-done.10.f2) | copy-start | bytes 3145732
  153.4 24.1 %copy-start.3 = (f32[2048,128]{1,0:T(8,128)S(1)}, f32[2048,128]{1,0:T(8,128)}, u32[]{:S(2)}) copy-start(f32[2048,128]{1,0:T(8,128)} %shard_map.43) | copy-start | bytes 3145732
  153.4 24.1 %collective-permute-start.15 = (f32[2048,128]{1,0:T(8,128)}, f32[2048,128]{1,0:T(8,128)S(1)}, u32[]{:S(2)}, u32[]{:S(2)}) collective-permute-start(f32[2048,128]{1,0:T(8,128)} %shard_map.43), channel_id=1, source_target_pairs={{0,2},{1,3},{2,0},{3,1},{4,6},{5,7},{6,4},{7,5},{8,10},{9,11},{10,... | collective-permute-start | bytes 3145736 | tf_op jit(solution)/shard_map/ppermute | solution.py:651
  177.6 8.0 %collective-permute-start.18 = (f32[2,2048,128]{2,1,0:T(8,128)S(1)}, f32[2,2048,128]{2,1,0:T(8,128)S(1)}, u32[]{:S(2)}, u32[]{:S(2)}) collective-permute-start(f32[2,2048,128]{2,1,0:T(8,128)S(1)} %pad_maximum_fusion.own.o0), channel_id=1, source_target_pairs={{0,1},{1,0},{2,3},{3,2},{4,5},{5,4},{6,7},{7,6},{8,9},{9,8},{10,11... | collective-permute-start | bytes 6291464 | tf_op jit(solution)/shard_map/ppermute | solution.py:651
  181.0 8.2 %collective-permute-start.22 = (f32[8,2,128,128]{3,2,1,0:T(8,128)S(1)}, f32[8,2,128,128]{3,2,1,0:T(8,128)S(1)}, u32[]{:S(2)}, u32[]{:S(2)}) collective-permute-start(f32[8,2,128,128]{3,2,1,0:T(8,128)S(1)} %copy-done.20), channel_id=1, source_target_pairs={{0,1},{1,0},{2,3},{3,2},{4,5},{5,4},{6,7},{7,6},{8,9},{9,8},{10,11... | collective-permute-start | bytes 3145736 | tf_op jit(solution)/shard_map/ppermute | solution.py:651
  183.6 33.2 %collective-permute-start.16 = (f32[2,1536,128]{2,1,0:T(8,128)}, f32[2,1536,128]{2,1,0:T(8,128)S(1)}, u32[]{:S(2)}, u32[]{:S(2)}) collective-permute-start(f32[2,1536,128]{2,1,0:T(8,128)} %fusion), channel_id=1, source_target_pairs={{0,4},{5,9},{10,14},{15,3},{16,20},{21,25},{26,30},{31,19},{32,36}... | collective-permute-start | bytes 4718600 | tf_op jit(solution)/shard_map/ppermute | solution.py:651
  184.4 32.5 %collective-permute-start.17 = (f32[2,1536,128]{2,1,0:T(8,128)}, f32[2,1536,128]{2,1,0:T(8,128)S(1)}, u32[]{:S(2)}, u32[]{:S(2)}) collective-permute-start(f32[2,1536,128]{2,1,0:T(8,128)} %fusion), channel_id=1, source_target_pairs={{0,12},{5,1},{10,6},{15,11},{16,28},{21,17},{26,22},{31,27},{32,44... | collective-permute-start | bytes 4718600 | tf_op jit(solution)/shard_map/ppermute | solution.py:651
  187.1 30.8 %collective-permute-start.19 = (f32[2,1536,128]{2,1,0:T(8,128)}, f32[2,1536,128]{2,1,0:T(8,128)S(1)}, u32[]{:S(2)}, u32[]{:S(2)}) collective-permute-start(f32[2,1536,128]{2,1,0:T(8,128)} %slice.42), channel_id=1, source_target_pairs={{0,4},{5,9},{10,14},{15,3},{16,20},{21,25},{26,30},{31,19},{32,36}... | collective-permute-start | bytes 4718600 | tf_op jit(solution)/shard_map/ppermute | solution.py:651
  187.8 37.4 %collective-permute-start.20 = (f32[2,1536,128]{2,1,0:T(8,128)}, f32[2,1536,128]{2,1,0:T(8,128)}, u32[]{:S(2)}, u32[]{:S(2)}) collective-permute-start(f32[2,1536,128]{2,1,0:T(8,128)} %slice.42), channel_id=1, source_target_pairs={{0,12},{5,1},{10,6},{15,11},{16,28},{21,17},{26,22},{31,27},{32,44... | collective-permute-start | bytes 4718600 | tf_op jit(solution)/shard_map/ppermute | solution.py:651
  189.2 21.3 %collective-permute-start.23 = (f32[8,2,128,128]{3,2,1,0:T(8,128)}, f32[8,2,128,128]{3,2,1,0:T(8,128)}, u32[]{:S(2)}, u32[]{:S(2)}) collective-permute-start(f32[8,2,128,128]{3,2,1,0:T(8,128)} %get-tuple-element.109), channel_id=1, source_target_pairs={{0,2},{1,3},{2,0},{3,1},{4,6},{5,7},{6,4},{7,5},{8,10},{9,11},{10,... | collective-permute-start | bytes 3145736 | tf_op jit(solution)/shard_map/ppermute | solution.py:651
  210.5 7.4 %collective-permute-start.21 = (f32[8,128]{1,0:T(8,128)}, f32[8,128]{1,0:T(8,128)S(1)}, u32[]{:S(2)}, u32[]{:S(2)}) collective-permute-start(f32[8,128]{1,0:T(8,128)} %get-tuple-element.107), channel_id=1, source_target_pairs={{0,1},{1,0},{2,3},{3,2},{4,5},{5,4},{6,7},{7,6},{8,9},{9,8},{10,11... | collective-permute-start | bytes 12296 | tf_op jit(solution)/shard_map/ppermute | solution.py:651
  225.2 29.3 %collective-permute-start.25 = (f32[2,1536,128]{2,1,0:T(8,128)S(1)}, f32[2,1536,128]{2,1,0:T(8,128)S(1)}, u32[]{:S(2)}, u32[]{:S(2)}) collective-permute-start(f32[2,1536,128]{2,1,0:T(8,128)S(1)} %collective-permute-done.16.o1), channel_id=1, source_target_pairs={{3,7},{4,8},{9,13},{14,2},{19,23},{20,24},{25,29},{30,18},{35,39},... | collective-permute-start | bytes 4718600 | tf_op jit(solution)/shard_map/ppermute | solution.py:651
  226.0 28.6 %collective-permute-start.26 = (f32[2,1536,128]{2,1,0:T(8,128)}, f32[2,1536,128]{2,1,0:T(8,128)}, u32[]{:S(2)}, u32[]{:S(2)}) collective-permute-start(f32[2,1536,128]{2,1,0:T(8,128)} %collective-permute-done.20.g3), channel_id=1, source_target_pairs={{1,13},{6,2},{11,7},{12,8},{17,29},{22,18},{27,23},{28,24},{33,45}... | collective-permute-start | bytes 4718600 | tf_op jit(solution)/shard_map/ppermute | solution.py:651
  228.4 26.1 %collective-permute-start.27 = (f32[8,2,128,128]{3,2,1,0:T(8,128)}, f32[8,2,128,128]{3,2,1,0:T(8,128)S(1)}, u32[]{:S(2)}, u32[]{:S(2)}) collective-permute-start(f32[8,2,128,128]{3,2,1,0:T(8,128)} %get-tuple-element.119), channel_id=1, source_target_pairs={{0,3},{1,2},{2,1},{3,0},{4,7},{5,6},{6,5},{7,4},{8,11},{9,10},{10,... | collective-permute-start | bytes 3145736 | tf_op jit(solution)/shard_map/ppermute | solution.py:651
  239.2 15.3 %collective-permute-start.24 = (f32[8,128]{1,0:T(8,128)}, f32[8,128]{1,0:T(8,128)S(1)}, u32[]{:S(2)}, u32[]{:S(2)}) collective-permute-start(f32[8,128]{1,0:T(8,128)} %get-tuple-element.116), channel_id=1, source_target_pairs={{0,1},{1,0},{2,3},{3,2},{4,5},{5,4},{6,7},{7,6},{8,9},{9,8},{10,11... | collective-permute-start | bytes 12296 | tf_op jit(solution)/shard_map/ppermute | solution.py:651
  (19 other events, 173.9 us)
